TPU v7x, 128 devices: a whole 4x4x4 slice. The times are simulated.
128 devices in a mesh: blk: 16 (over z, y_lo, core), quad: 8 (over y_hi, x).
Axes of the slice: x: 4, y: 4 (y_hi: 2, y_lo: 2; y = y_hi * 2 + y_lo), z: 4, core: 2. Of those that a mesh axis runs over, the one named last changes fastest.
Arguments:
- positions: bfloat16 [3, 65536], P(None, ('blk', 'quad')), may hold values from -1 to 1
- normals: bfloat16 [3, 65536], P(None, ('blk', 'quad')), may hold values from -1 to 1, as said below
- patch_area: bfloat16 [65536], P(('blk', 'quad')), may hold values from 0.00048828125 to 0.00390625
- reflect: float32 [65536], P(('blk', 'quad')), may hold values from 0.3 to 0.9
- emission: float32 [65536, 128], P(('blk', 'quad')), may hold values from 0.1 to 1
- radiosity: float32 [65536, 128], P(('blk', 'quad')), may hold values from 0.2 to 2
- visible: int32 [512, 512], P('blk'), may hold values from 0 to 1, as said below
Outputs:
- updated: float32 [65536, 128], P(('blk', 'quad'))
Inputs may be any that keep to these rules, and one draw needn't show every extreme that they name: Each column of normals has unit length up to rounding to bfloat16. visible[a, b] equals visible[b, a].
All inputs are finite; a program needn't handle non-finite values.
Results may differ from a plain program's by a relative error of at most 0.0003.
Values may be sent and summed in bfloat16 or wider, within the bound.
No kernel may reach another device: no remote copies, remote signals or barrier semaphores. Data moves between devices by JAX's collectives and lax.ppermute only.
A program may use at most 128 MiB of HBM per device.

v0:
```python
import math

import jax
import jax.numpy as jnp
from jax import lax
from jax.sharding import PartitionSpec as P


def from_behind(value, axis, steps):
    count = lax.axis_size(axis)
    pairs = [(source, (source + steps) % count) for source in range(count)]
    return lax.ppermute(value, axis, pairs)


def kernel_tile(row_geometry, col_geometry):
    delta_x = col_geometry[0][None, :] - row_geometry[0][:, None]
    delta_y = col_geometry[1][None, :] - row_geometry[1][:, None]
    delta_z = col_geometry[2][None, :] - row_geometry[2][:, None]
    facing_row = jnp.maximum(
        row_geometry[3][:, None] * delta_x
        + row_geometry[4][:, None] * delta_y
        + row_geometry[5][:, None] * delta_z,
        0.0,
    )
    facing_col = jnp.maximum(
        -(
            col_geometry[3][None, :] * delta_x
            + col_geometry[4][None, :] * delta_y
            + col_geometry[5][None, :] * delta_z
        ),
        0.0,
    )
    distance = delta_x * delta_x + delta_y * delta_y + delta_z * delta_z
    denominator = distance + (row_geometry[6][:, None] + col_geometry[6][None, :])
    return facing_row * facing_col / (math.pi * denominator * denominator)


def pair_terms(
    block_geom, block_ab, far_geom, far_weighted, tile_masks, tile_side, band_rows, two_sided
):
    block_len = block_ab.shape[0]
    sub_size = far_weighted.shape[0]
    num_cases = far_weighted.shape[1]
    band_count = block_len // band_rows
    band_geoms = block_geom.reshape(7, band_count, band_rows).transpose(1, 0, 2)
    band_abs = block_ab.reshape(band_count, band_rows, num_cases)
    band_masks = tile_masks.reshape(band_count, band_rows // tile_side, sub_size // tile_side)

    def compute(band_geom, band_ab, band_mask):
        kernel = kernel_tile(band_geom, far_geom)
        shaped = kernel.reshape(
            band_rows // tile_side, tile_side, sub_size // tile_side, tile_side
        ) * band_mask[:, None, :, None].astype(jnp.float32)
        coupling = shaped.reshape(band_rows, sub_size).astype(jnp.bfloat16)
        row_terms = jnp.dot(coupling, far_weighted, preferred_element_type=jnp.float32)
        if two_sided:
            col_terms = lax.dot_general(
                coupling, band_ab, (((0,), (0,)), ((), ())), preferred_element_type=jnp.float32
            )
        else:
            col_terms = jnp.zeros((sub_size, num_cases), jnp.float32)
        return (row_terms, col_terms)

    def band_step(col_running, items):
        band_geom, band_ab, band_mask = items
        row_terms, col_terms = compute(band_geom, band_ab, band_mask)
        return (col_running + col_terms, row_terms)

    col_total, row_stack = lax.scan(
        band_step, jnp.zeros((sub_size, num_cases), jnp.float32), (band_geoms, band_abs, band_masks)
    )
    return (row_stack.reshape(block_len, num_cases), col_total)


def shards(positions, normals, patch_area, reflect, emission, radiosity, visible):
    sub_size = patch_area.shape[0]
    num_cases = radiosity.shape[1]
    blk_count = lax.axis_size("blk")
    quad_count = lax.axis_size("quad")
    block_len = sub_size * quad_count
    tile_side = block_len // visible.shape[0]
    band_rows = min(512, block_len)
    half_loop = blk_count // 2
    geometry = jnp.concatenate([positions, normals, patch_area[None, :]], 0)
    weighted = (patch_area.astype(jnp.float32)[:, None] * radiosity).astype(jnp.bfloat16)
    block_geom, block_ab = (
        lax.all_gather(geometry, "quad", axis=1, tiled=True),
        lax.all_gather(weighted, "quad", axis=0, tiled=True),
    )
    block_geom = block_geom.astype(jnp.float32)
    blk_index = lax.axis_index("blk")
    sub_index = lax.axis_index("quad")

    def visit(far_geom, far_weighted, offset, two_sided):
        partner = (blk_index - offset + blk_count) % blk_count
        col_start = (partner * block_len + sub_index * sub_size) // tile_side
        tile_masks = lax.dynamic_slice_in_dim(visible, col_start, sub_size // tile_side, 1)
        return pair_terms(
            block_geom,
            block_ab,
            far_geom.astype(jnp.float32),
            far_weighted,
            tile_masks,
            tile_side,
            band_rows,
            two_sided,
        )

    rows_total, _ = visit(geometry, weighted, 0, False)
    returned = jnp.zeros((sub_size, num_cases), jnp.float32)
    for offset in range(1, half_loop + 1):
        far_geom, far_weighted = from_behind((geometry, weighted), "blk", offset)
        row_terms, col_terms = visit(far_geom, far_weighted, offset, offset < half_loop)
        rows_total = rows_total + row_terms
        if offset < half_loop:
            returned = returned + from_behind(col_terms, "blk", -offset)
    own_part = lax.psum_scatter(rows_total, "quad", scatter_dimension=0, tiled=True)
    irradiation = own_part + returned
    return emission + reflect[:, None] * irradiation


def solution(mesh):
    in_specs = (
        P(None, ("blk", "quad")),
        P(None, ("blk", "quad")),
        P(("blk", "quad")),
        P(("blk", "quad")),
        P(("blk", "quad"), None),
        P(("blk", "quad"), None),
        P("blk", None),
    )
    out_specs = P(("blk", "quad"), None)
    return jax.shard_map(shards, mesh=mesh, in_specs=in_specs, out_specs=out_specs, check_vma=False)
```

profile of v0, /device:TPU:1, one launch (start us, length us, event | category | flops | bytes accessed | tf_op | source)
XLA Modules:
  0.0 796.7 jit_solution(15674966755537963687)
XLA Ops:
  20.1 28.6 %all_gather.6 = bf16[7,4096]{1,0:T(8,128)(2,1)S(1)} all-gather(bf16[7,512]{1,0:T(8,128)(2,1)} %get-tuple-element.848), channel_id=1, replica_groups=mesh['blk'=16,'quad'=8] {'quad'}, dimensions={1}, use_global_device_ids=true | all-gather | bytes 64512 | tf_op jit(solution)/shard_map/all_gather | solution.py:87
  52.0 7.4 collective-permute-start.12
  62.6 20.1 %while.111 = (s32[]{:T(128)}, f32[8,512,128]{2,1,0:T(8,128)S(1)}, f32[8,7,512]{2,1,0:T(8,128)S(1)}, f32[7,512]{1,0:T(8,128)S(1)}, s32[8,4,4]{2,1,0:T(4,128)S(1)}...) while((s32[]{:T(128)}, f32[8,512,128]{2,1,0:T(8,128)S(1)}, ...), condition=%wide.region_1.2_spmd, body=%wide.region_0.1_spmd.sunk | while | flops 74711064 | bytes 2576817 | solution.py:69
  97.5 42.2 %while.112 = (s32[]{:T(128)}, f32[8,512,128]{2,1,0:T(8,128)}, f32[8,7,512]{2,1,0:T(8,128)S(1)}, f32[7,512]{1,0:T(8,128)}, s32[8,4,4]{2,1,0:T(4,128)}, /*index=5*...) while((s32[]{:T(128)}, f32[8,512,128]{2,1,0:T(8,128)}, ...), condition=%wide.region_17.18_spmd, body=%wide.region_16.17_spmd.sunk | while | flops 74711064 | bytes 2577325 | solution.py:69
  143.1 72.4 %while.113 = (s32[]{:T(128)}, f32[512,128]{1,0:T(8,128)S(1)}, f32[8,512,128]{2,1,0:T(8,128)}, f32[8,7,512]{2,1,0:T(8,128)S(1)}, f32[7,512]{1,0:T(8,128)S(1)}, /*...) while((s32[]{:T(128)}, f32[512,128]{1,0:T(8,128)S(1)}, ...), condition=%wide.region_3.4_spmd.clone, body=%wide.region_2.3_spmd.clone.sunk | while | flops 149553184 | bytes 4310027 | solution.py:69
  147.3 4.5 fusion.558
  156.3 4.5 fusion.558
  165.4 4.5 fusion.558
  174.4 4.5 fusion.558
  183.5 4.5 fusion.558
  192.5 4.5 fusion.558
  201.6 4.5 fusion.558
  210.7 4.5 fusion.558
  218.5 80.2 %while.114 = (s32[]{:T(128)}, f32[512,128]{1,0:T(8,128)S(1)}, f32[8,512,128]{2,1,0:T(8,128)}, f32[8,7,512]{2,1,0:T(8,128)S(1)}, f32[7,512]{1,0:T(8,128)}, /*inde...) while((s32[]{:T(128)}, f32[512,128]{1,0:T(8,128)S(1)}, ...), condition=%wide.region_5.6_spmd.clone, body=%wide.region_4.5_spmd.clone.sunk | while | flops 149553184 | bytes 4310027 | solution.py:69
  223.6 4.5 fusion.566
  233.6 4.5 fusion.566
  243.7 4.5 fusion.566
  253.7 4.5 fusion.566
  263.7 4.5 fusion.566
  273.7 4.5 fusion.566
  283.7 4.5 fusion.566
  293.8 4.5 fusion.566
  300.2 81.7 %while.115 = (s32[]{:T(128)}, f32[512,128]{1,0:T(8,128)S(1)}, f32[8,512,128]{2,1,0:T(8,128)}, f32[8,7,512]{2,1,0:T(8,128)S(1)}, f32[7,512]{1,0:T(8,128)}, /*inde...) while((s32[]{:T(128)}, f32[512,128]{1,0:T(8,128)S(1)}, ...), condition=%wide.region_7.8_spmd.clone, body=%wide.region_6.7_spmd.clone.sunk | while | flops 149553184 | bytes 4310027 | solution.py:69
  305.5 4.5 fusion.574
  315.7 4.5 fusion.574
  325.9 4.5 fusion.574
  336.1 4.5 fusion.574
  346.3 4.5 fusion.574
  356.6 4.5 fusion.574
  366.8 4.5 fusion.574
  377.0 4.5 fusion.574
  383.4 80.2 %while.116 = (s32[]{:T(128)}, f32[512,128]{1,0:T(8,128)S(1)}, f32[8,512,128]{2,1,0:T(8,128)}, f32[8,7,512]{2,1,0:T(8,128)S(1)}, f32[7,512]{1,0:T(8,128)}, /*inde...) while((s32[]{:T(128)}, f32[512,128]{1,0:T(8,128)S(1)}, ...), condition=%wide.region_9.10_spmd.clone, body=%wide.region_8.9_spmd.clone.sunk | while | flops 149553184 | bytes 4310027 | solution.py:69
  388.5 4.5 fusion.582
  398.5 4.5 fusion.582
  408.6 4.5 fusion.582
  418.6 4.5 fusion.582
  428.6 4.5 fusion.582
  438.6 4.5 fusion.582
  448.7 4.5 fusion.582
  458.7 4.5 fusion.582
  465.1 80.2 %while.117 = (s32[]{:T(128)}, f32[512,128]{1,0:T(8,128)S(1)}, f32[8,512,128]{2,1,0:T(8,128)}, f32[8,7,512]{2,1,0:T(8,128)S(1)}, f32[7,512]{1,0:T(8,128)}, /*inde...) while((s32[]{:T(128)}, f32[512,128]{1,0:T(8,128)S(1)}, ...), condition=%wide.region_11.12_spmd.clone, body=%wide.region_10.11_spmd.clone.sunk | while | flops 149553184 | bytes 4310027 | solution.py:69
  470.2 4.5 fusion.590
  480.2 4.5 fusion.590
  490.2 4.5 fusion.590
  500.2 4.5 fusion.590
  510.3 4.5 fusion.590
  520.3 4.5 fusion.590
  530.3 4.5 fusion.590
  540.3 4.5 fusion.590
  546.9 80.2 %while.118 = (s32[]{:T(128)}, f32[512,128]{1,0:T(8,128)S(1)}, f32[8,512,128]{2,1,0:T(8,128)}, f32[8,7,512]{2,1,0:T(8,128)S(1)}, f32[7,512]{1,0:T(8,128)}, /*inde...) while((s32[]{:T(128)}, f32[512,128]{1,0:T(8,128)S(1)}, ...), condition=%wide.region_13.14_spmd.clone, body=%wide.region_12.13_spmd.clone.sunk | while | flops 149553184 | bytes 4310027 | solution.py:69
  552.0 4.5 fusion.598
  562.0 4.5 fusion.598
  571.9 4.5 fusion.598
  582.0 4.5 fusion.598
  592.0 4.5 fusion.598
  602.0 4.5 fusion.598
  612.1 4.5 fusion.598
  622.1 4.5 fusion.598
  628.5 72.4 %while.119 = (s32[]{:T(128)}, f32[512,128]{1,0:T(8,128)S(1)}, f32[8,512,128]{2,1,0:T(8,128)}, f32[8,7,512]{2,1,0:T(8,128)S(1)}, f32[7,512]{1,0:T(8,128)S(1)}, /*...) while((s32[]{:T(128)}, f32[512,128]{1,0:T(8,128)S(1)}, ...), condition=%wide.region_15.16_spmd.clone, body=%wide.region_14.15_spmd.clone.sunk | while | flops 149553184 | bytes 4310027 | solution.py:69
  687.0 4.5 fusion.606
  700.9 9.0 %add_add_fusion = f32[8,512,128]{2,1,0:T(8,128)} fusion(f32[8,512,128]{2,1,0:T(8,128)} %get-tuple-element.378, f32[8,512,128]{2,1,0:T(8,128)} %get-tuple-element.377, f32[8,512,128]{2,1,0:T(8,128)} %get-tuple-element.376, f32[8,512,128]{2,1,0:T(8,128)} %get-tuple-element.375, f32[8,512,128]{2,1,0:T(8,128)} %get-tuple-element.374, ...), kind=kLoop, calls=%fused_computation.696 | loop fusion | flops 4194304 | bytes 20971520 | tf_op jit(solution)/shard_map/add | solution.py:114
  723.2 8.7 %collective-permute-start.22 = (f32[512,128]{1,0:T(8,128)S(1)}, f32[512,128]{1,0:T(8,128)S(1)}, u32[]{:S(2)}, u32[]{:S(2)}) collective-permute-start(f32[512,128]{1,0:T(8,128)S(1)} %get-tuple-element.385), channel_id=1, source_target_pairs={{0,72},{8,80},{16,88},{24,96},{32,104},{40,112},{48,120},{56,0},{6... | collective-permute-start | bytes 786440 | tf_op jit(solution)/shard_map/ppermute | solution.py:12
  734.6 6.9 collective-permute-done.22
  741.5 46.6 %reduce-scatter.2.cloned.1.call-done = f32[512,128]{1,0:T(8,128)} async-done(((f32[4096,128]{1,0:T(8,128)}), f32[512,128]{1,0:T(8,128)}) %reduce-scatter.2.cloned.1.call-update) | async-done | bytes 262160 | tf_op jit(solution)/shard_map/reduce_scatter | solution.py:117
  (522 shorter events, 451.0 us)
Async XLA Ops:
  6.5 135.1 %all-gather.2.cloned.1.call-start = ((), (), s32[]{:S(2)}) async-start(), calls=%async_computation.1 | async-start | bytes 1179648 | tf_op jit(solution)/shard_map/all_gather | solution.py:88
  8.5 42.1 %collective-permute-start = (bf16[7,512]{1,0:T(8,128)(2,1)}, bf16[7,512]{1,0:T(8,128)(2,1)S(1)}, u32[]{:S(2)}, u32[]{:S(2)}) collective-permute-start(bf16[7,512]{1,0:T(8,128)(2,1)} %get-tuple-element.848), channel_id=1, source_target_pairs={{0,8},{8,16},{16,24},{24,32},{32,40},{40,48},{48,56},{56,64},{64,7... | collective-permute-start | bytes 21512 | tf_op jit(solution)/shard_map/ppermute | solution.py:12
  11.2 40.8 %collective-permute-start.2 = (bf16[7,512]{1,0:T(8,128)(2,1)}, bf16[7,512]{1,0:T(8,128)(2,1)S(1)}, u32[]{:S(2)}, u32[]{:S(2)}) collective-permute-start(bf16[7,512]{1,0:T(8,128)(2,1)} %get-tuple-element.848), channel_id=1, source_target_pairs={{0,16},{8,24},{16,32},{24,40},{32,48},{40,56},{48,64},{56,72},{64,... | collective-permute-start | bytes 21512 | tf_op jit(solution)/shard_map/ppermute | solution.py:12
  12.7 46.7 %collective-permute-start.4 = (bf16[7,512]{1,0:T(8,128)(2,1)}, bf16[7,512]{1,0:T(8,128)(2,1)S(1)}, u32[]{:S(2)}, u32[]{:S(2)}) collective-permute-start(bf16[7,512]{1,0:T(8,128)(2,1)} %get-tuple-element.848), channel_id=1, source_target_pairs={{0,24},{8,32},{16,40},{24,48},{32,56},{40,64},{48,72},{56,80},{64,... | collective-permute-start | bytes 21512 | tf_op jit(solution)/shard_map/ppermute | solution.py:12
  13.2 46.7 %collective-permute-start.6 = (bf16[7,512]{1,0:T(8,128)(2,1)}, bf16[7,512]{1,0:T(8,128)(2,1)S(1)}, u32[]{:S(2)}, u32[]{:S(2)}) collective-permute-start(bf16[7,512]{1,0:T(8,128)(2,1)} %get-tuple-element.848), channel_id=1, source_target_pairs={{0,32},{8,40},{16,48},{24,56},{32,64},{40,72},{48,80},{56,88},{64,... | collective-permute-start | bytes 21512 | tf_op jit(solution)/shard_map/ppermute | solution.py:12
  14.8 72.6 %collective-permute-start.8 = (bf16[7,512]{1,0:T(8,128)(2,1)}, bf16[7,512]{1,0:T(8,128)(2,1)S(1)}, u32[]{:S(2)}, u32[]{:S(2)}) collective-permute-start(bf16[7,512]{1,0:T(8,128)(2,1)} %get-tuple-element.848), channel_id=1, source_target_pairs={{0,40},{8,48},{16,56},{24,64},{32,72},{40,80},{48,88},{56,96},{64,... | collective-permute-start | bytes 21512 | tf_op jit(solution)/shard_map/ppermute | solution.py:12
  19.8 768.3 %reduce-scatter.2.cloned.1.call-start = ((), (), s32[]{:S(2)}) async-start(), calls=%async_computation.2 | async-start | bytes 2359296 | tf_op jit(solution)/shard_map/reduce_scatter | solution.py:117
  50.7 37.3 %collective-permute-start.10 = (bf16[7,512]{1,0:T(8,128)(2,1)}, bf16[7,512]{1,0:T(8,128)(2,1)}, u32[]{:S(2)}, u32[]{:S(2)}) collective-permute-start(bf16[7,512]{1,0:T(8,128)(2,1)} %get-tuple-element.848), channel_id=1, source_target_pairs={{0,48},{8,56},{16,64},{24,72},{32,80},{40,88},{48,96},{56,104},{64... | collective-permute-start | bytes 21512 | tf_op jit(solution)/shard_map/ppermute | solution.py:12
  52.0 10.5 %copy-start.6 = (bf16[7,512]{1,0:T(8,128)(2,1)}, bf16[7,512]{1,0:T(8,128)(2,1)S(1)}, u32[]{:S(2)}) copy-start(bf16[7,512]{1,0:T(8,128)(2,1)S(1)} %collective-permute-done.2) | copy-start | bytes 21508
  52.0 38.3 %collective-permute-start.12 = (bf16[7,512]{1,0:T(8,128)(2,1)}, bf16[7,512]{1,0:T(8,128)(2,1)}, u32[]{:S(2)}, u32[]{:S(2)}) collective-permute-start(bf16[7,512]{1,0:T(8,128)(2,1)} %get-tuple-element.848), channel_id=1, source_target_pairs={{0,56},{8,64},{16,72},{24,80},{32,88},{40,96},{48,104},{56,112},{6... | collective-permute-start | bytes 21512 | tf_op jit(solution)/shard_map/ppermute | solution.py:12
  59.4 3.1 copy-start.7
  59.4 34.6 %collective-permute-start.15 = (bf16[512,128]{1,0:T(8,128)(2,1)}, bf16[512,128]{1,0:T(8,128)(2,1)}, u32[]{:S(2)}, u32[]{:S(2)}) collective-permute-start(bf16[512,128]{1,0:T(8,128)(2,1)} %multiply_convert_fusion), channel_id=1, source_target_pairs={{0,64},{8,72},{16,80},{24,88},{32,96},{40,104},{48,112},{56,120},{... | collective-permute-start | bytes 393224 | tf_op jit(solution)/shard_map/ppermute | solution.py:12
  59.9 2.7 copy-start.8
  59.9 32.8 %collective-permute-start.14 = (bf16[7,512]{1,0:T(8,128)(2,1)}, bf16[7,512]{1,0:T(8,128)(2,1)}, u32[]{:S(2)}, u32[]{:S(2)}) collective-permute-start(bf16[7,512]{1,0:T(8,128)(2,1)} %get-tuple-element.848), channel_id=1, source_target_pairs={{0,64},{8,72},{16,80},{24,88},{32,96},{40,104},{48,112},{56,120},{... | collective-permute-start | bytes 21512 | tf_op jit(solution)/shard_map/ppermute | solution.py:12
  82.7 14.8 %copy-start.1 = (f32[8,512,128]{2,1,0:T(8,128)}, f32[8,512,128]{2,1,0:T(8,128)S(1)}, u32[]{:S(2)}) copy-start(f32[8,512,128]{2,1,0:T(8,128)S(1)} %get-tuple-element.370) | copy-start | bytes 6291460
  87.4 52.3 %collective-permute-start.1 = (bf16[512,128]{1,0:T(8,128)(2,1)}, bf16[512,128]{1,0:T(8,128)(2,1)}, u32[]{:S(2)}, u32[]{:S(2)}) collective-permute-start(bf16[512,128]{1,0:T(8,128)(2,1)} %multiply_convert_fusion), channel_id=1, source_target_pairs={{0,8},{8,16},{16,24},{24,32},{32,40},{40,48},{48,56},{56,64},{64,7... | collective-permute-start | bytes 393224 | tf_op jit(solution)/shard_map/ppermute | solution.py:12
  88.0 127.6 %collective-permute-start.3 = (bf16[512,128]{1,0:T(8,128)(2,1)}, bf16[512,128]{1,0:T(8,128)(2,1)}, u32[]{:S(2)}, u32[]{:S(2)}) collective-permute-start(bf16[512,128]{1,0:T(8,128)(2,1)} %multiply_convert_fusion), channel_id=1, source_target_pairs={{0,16},{8,24},{16,32},{24,40},{32,48},{40,56},{48,64},{56,72},{64,... | collective-permute-start | bytes 393224 | tf_op jit(solution)/shard_map/ppermute | solution.py:12
  90.4 208.3 %collective-permute-start.5 = (bf16[512,128]{1,0:T(8,128)(2,1)}, bf16[512,128]{1,0:T(8,128)(2,1)}, u32[]{:S(2)}, u32[]{:S(2)}) collective-permute-start(bf16[512,128]{1,0:T(8,128)(2,1)} %multiply_convert_fusion), channel_id=1, source_target_pairs={{0,24},{8,32},{16,40},{24,48},{32,56},{40,64},{48,72},{56,80},{64,... | collective-permute-start | bytes 393224 | tf_op jit(solution)/shard_map/ppermute | solution.py:12
  92.7 289.2 %collective-permute-start.7 = (bf16[512,128]{1,0:T(8,128)(2,1)}, bf16[512,128]{1,0:T(8,128)(2,1)}, u32[]{:S(2)}, u32[]{:S(2)}) collective-permute-start(bf16[512,128]{1,0:T(8,128)(2,1)} %multiply_convert_fusion), channel_id=1, source_target_pairs={{0,32},{8,40},{16,48},{24,56},{32,64},{40,72},{48,80},{56,88},{64,... | collective-permute-start | bytes 393224 | tf_op jit(solution)/shard_map/ppermute | solution.py:12
  94.0 369.6 %collective-permute-start.9 = (bf16[512,128]{1,0:T(8,128)(2,1)}, bf16[512,128]{1,0:T(8,128)(2,1)}, u32[]{:S(2)}, u32[]{:S(2)}) collective-permute-start(bf16[512,128]{1,0:T(8,128)(2,1)} %multiply_convert_fusion), channel_id=1, source_target_pairs={{0,40},{8,48},{16,56},{24,64},{32,72},{40,80},{48,88},{56,96},{64,... | collective-permute-start | bytes 393224 | tf_op jit(solution)/shard_map/ppermute | solution.py:12
  139.7 3.5 copy-start.3
  139.7 3.5 copy-start.4
  139.7 405.6 %collective-permute-start.11 = (bf16[512,128]{1,0:T(8,128)(2,1)}, bf16[512,128]{1,0:T(8,128)(2,1)}, u32[]{:S(2)}, u32[]{:S(2)}) collective-permute-start(bf16[512,128]{1,0:T(8,128)(2,1)} %multiply_convert_fusion), channel_id=1, source_target_pairs={{0,48},{8,56},{16,64},{24,72},{32,80},{40,88},{48,96},{56,104},{64... | collective-permute-start | bytes 393224 | tf_op jit(solution)/shard_map/ppermute | solution.py:12
  141.6 1.5 copy-start
  215.6 2.9 copy-start.2
  215.6 411.4 %collective-permute-start.13 = (bf16[512,128]{1,0:T(8,128)(2,1)}, bf16[512,128]{1,0:T(8,128)(2,1)}, u32[]{:S(2)}, u32[]{:S(2)}) collective-permute-start(bf16[512,128]{1,0:T(8,128)(2,1)} %multiply_convert_fusion), channel_id=1, source_target_pairs={{0,56},{8,64},{16,72},{24,80},{32,88},{40,96},{48,104},{56,112},{6... | collective-permute-start | bytes 393224 | tf_op jit(solution)/shard_map/ppermute | solution.py:12
  709.9 78.1 %copy-start.5 = (f32[512,128]{1,0:T(8,128)S(1)}, f32[512,128]{1,0:T(8,128)}, u32[]{:S(2)}) copy-start(f32[512,128]{1,0:T(8,128)} %param.29) | copy-start | bytes 786436
  709.9 78.1 %copy-start.9 = (f32[512]{0:T(512)S(1)}, f32[512]{0:T(512)}, u32[]{:S(2)}) copy-start(f32[512]{0:T(512)} %param.28) | copy-start | bytes 6148
  710.0 10.2 %collective-permute-start.16 = (f32[512,128]{1,0:T(8,128)S(1)}, f32[512,128]{1,0:T(8,128)S(1)}, u32[]{:S(2)}, u32[]{:S(2)}) collective-permute-start(f32[512,128]{1,0:T(8,128)S(1)} %get-tuple-element.379), channel_id=1, source_target_pairs={{0,120},{8,0},{16,8},{24,16},{32,24},{40,32},{48,40},{56,48},{64,5... | collective-permute-start | bytes 786440 | tf_op jit(solution)/shard_map/ppermute | solution.py:12
  711.0 12.2 %collective-permute-start.17 = (f32[512,128]{1,0:T(8,128)S(1)}, f32[512,128]{1,0:T(8,128)S(1)}, u32[]{:S(2)}, u32[]{:S(2)}) collective-permute-start(f32[512,128]{1,0:T(8,128)S(1)} %get-tuple-element.380), channel_id=1, source_target_pairs={{0,112},{8,120},{16,0},{24,8},{32,16},{40,24},{48,32},{56,40},{64,... | collective-permute-start | bytes 786440 | tf_op jit(solution)/shard_map/ppermute | solution.py:12
  712.8 19.1 %collective-permute-start.18 = (f32[512,128]{1,0:T(8,128)S(1)}, f32[512,128]{1,0:T(8,128)S(1)}, u32[]{:S(2)}, u32[]{:S(2)}) collective-permute-start(f32[512,128]{1,0:T(8,128)S(1)} %get-tuple-element.381), channel_id=1, source_target_pairs={{0,104},{8,112},{16,120},{24,0},{32,8},{40,16},{48,24},{56,32},{64... | collective-permute-start | bytes 786440 | tf_op jit(solution)/shard_map/ppermute | solution.py:12
  715.4 16.4 %collective-permute-start.19 = (f32[512,128]{1,0:T(8,128)S(1)}, f32[512,128]{1,0:T(8,128)S(1)}, u32[]{:S(2)}, u32[]{:S(2)}) collective-permute-start(f32[512,128]{1,0:T(8,128)S(1)} %get-tuple-element.382), channel_id=1, source_target_pairs={{0,96},{8,104},{16,112},{24,120},{32,0},{40,8},{48,16},{56,24},{64... | collective-permute-start | bytes 786440 | tf_op jit(solution)/shard_map/ppermute | solution.py:12
  715.9 18.6 %collective-permute-start.20 = (f32[512,128]{1,0:T(8,128)S(1)}, f32[512,128]{1,0:T(8,128)S(1)}, u32[]{:S(2)}, u32[]{:S(2)}) collective-permute-start(f32[512,128]{1,0:T(8,128)S(1)} %get-tuple-element.383), channel_id=1, source_target_pairs={{0,88},{8,96},{16,104},{24,112},{32,120},{40,0},{48,8},{56,16},{64... | collective-permute-start | bytes 786440 | tf_op jit(solution)/shard_map/ppermute | solution.py:12
  720.2 14.4 %collective-permute-start.21 = (f32[512,128]{1,0:T(8,128)S(1)}, f32[512,128]{1,0:T(8,128)S(1)}, u32[]{:S(2)}, u32[]{:S(2)}) collective-permute-start(f32[512,128]{1,0:T(8,128)S(1)} %get-tuple-element.384), channel_id=1, source_target_pairs={{0,80},{8,88},{16,96},{24,104},{32,112},{40,120},{48,0},{56,8},{64... | collective-permute-start | bytes 786440 | tf_op jit(solution)/shard_map/ppermute | solution.py:12
  723.2 18.3 %collective-permute-start.22 = (f32[512,128]{1,0:T(8,128)S(1)}, f32[512,128]{1,0:T(8,128)S(1)}, u32[]{:S(2)}, u32[]{:S(2)}) collective-permute-start(f32[512,128]{1,0:T(8,128)S(1)} %get-tuple-element.385), channel_id=1, source_target_pairs={{0,72},{8,80},{16,88},{24,96},{32,104},{40,112},{48,120},{56,0},{6... | collective-permute-start | bytes 786440 | tf_op jit(solution)/shard_map/ppermute | solution.py:12
Sparse Core Ops, SparseCore 0:
  19.9 47.2 all-gather.1
  710.1 77.9 reduce-scatter.1
where the time goes:
time: 805 us; the launch traced here: 797 us
  other arithmetic  319 us (40%)
  matrix products  242 us (30%)
  local copies, waits for them, and re-layouts  82.5 us (10%)
  waiting for transfers between devices  59.5 us (7%)
  starting transfers between devices  47.2 us (6%)
  blocking collectives  28.6 us (4%)
  between operations  14 us (2%)
    convert_element_type x56, other arithmetic, compute(): coupling = shaped.reshape(band_rows, sub_size).astype(jnp.bfloat16)  253 us
    dot_general x72, matrix products, compute(): jnp.dot(coupling, far_weighted, preferred_element_type=jnp.float32)  221 us
    slice x72, local copies, waits for them, and re-layouts, kernel_tile(): delta_x = col_geometry[0][None, :] - row_geometry[0][:, None]  50.8 us
    ppermute x23, starting transfers between devices, from_behind(): return lax.ppermute(value, axis, pairs)  47.1 us
    reduce_scatter x1, waiting for transfers between devices, shards(): lax.psum_scatter(rows_total, 'quad', scatter_dimension=0, tiled=True)  46.6 us
    convert_element_type x72, other arithmetic, compute(): band_mask[:, None, :, None].astype(jnp.float32)  43.5 us
    all_gather x1, blocking collectives, shards(): lax.all_gather(geometry, 'quad', axis=1, tiled=True)  28.6 us
    dot_general x56, matrix products, compute(): lax.dot_general(coupling, band_ab, (((0,), (0,)), ((), ())), preferred_el...  21.1 us
  transfers between devices with their start and end apart: 25, of which 4 were waited for; matrix products, arithmetic and copies ran while one was open for 70% of the time, Pallas kernels for 0%

commit v1 on v0

v1 whole, which is shorter than its diff:
```python
import functools
import math

import numpy as np

import jax
import jax.numpy as jnp
from jax import lax
from jax.experimental import pallas as pl
from jax.experimental.pallas import tpu as pltpu
from jax.sharding import PartitionSpec as P

BF16, F32 = jnp.bfloat16, jnp.float32
AXES = ("blk", "quad")
SUB = 512
TILE = 128
CASES = 128
TILES = SUB // TILE
GEOM = 16 * TILES
MSG = SUB + GEOM
SLOTS = 64
MASK = 32
CHUNK = 512
ROWS = 1024
VMEM = 56 << 20

SIZE, ALONG, ONES = 8, 11, 14
PARTS = 32


def expansions():
    den, face_row, face_col = (np.zeros((128, SLOTS), np.float32) for _ in range(3))
    for i in range(3):
        den[i, i] = -2
        den[ONES, SIZE + i] = 1
        den[SIZE + i, ONES + i] = 1
        face_row[3 + i, i] = 1
        face_row[ALONG + i, ONES + i] = -1
        face_col[i, 3 + i] = 1
        face_col[ONES, ALONG + i] = -1
    return np.stack([den, face_row, face_col])


def params(**kw):
    return pltpu.CompilerParams(vmem_limit_bytes=VMEM, **kw)


def message_kernel(pos, nrm, area, rad, vis, msg, geom, buf):
    quad = lax.axis_index("quad")
    buf[...] = jnp.zeros_like(buf)
    rows = jnp.zeros((TILES, vis.shape[1]), F32)
    for q in range(vis.shape[0] // TILES):
        part = vis[q * TILES : (q + 1) * TILES, :].astype(F32)
        rows = rows + jnp.where(quad == q, 1.0, 0.0) * part
    for t in range(TILES):
        cols = slice(t * TILE, (t + 1) * TILE)
        buf[16 * t : 16 * t + 3, :] = pos[:, cols].astype(F32)
        buf[16 * t + 3 : 16 * t + 6, :] = nrm[:, cols].astype(F32)
        own = area[:, cols].astype(F32)
        buf[16 * t + 6 : 16 * t + 7, :] = own
        for k in range(vis.shape[1] // TILE):
            buf[16 * t + 8 + k : 16 * t + 9 + k, :] = rows[t : t + 1, k * TILE : (k + 1) * TILE]
        lanes = jnp.broadcast_to(own, (TILE, TILE)).T
        msg[cols, :] = (lanes * rad[cols, :]).astype(BF16)
    packed = buf[...].astype(BF16)
    msg[SUB:, :] = packed
    geom[...] = packed


def make_message(pos, nrm, area, rad, vis):
    return pl.pallas_call(
        message_kernel,
        out_shape=(
            jax.ShapeDtypeStruct((MSG, CASES), BF16),
            jax.ShapeDtypeStruct((GEOM, TILE), BF16),
        ),
        scratch_shapes=[pltpu.VMEM((GEOM, TILE), F32)],
        compiler_params=params(),
    )(pos, nrm, area, rad, vis)


def write_parts(flat, parts):
    parts[...] = jnp.zeros_like(parts)
    parts[:8, :] = flat
    pos = [flat[i : i + 1, :] for i in range(3)]
    nrm = [flat[3 + i : 4 + i, :] for i in range(3)]
    size = pos[0] * pos[0] + pos[1] * pos[1] + pos[2] * pos[2] + flat[6:7, :]
    along = nrm[0] * pos[0] + nrm[1] * pos[1] + nrm[2] * pos[2]
    for first, rest in ((SIZE, size), (ALONG, along)):
        for k in range(3):
            part = rest.astype(BF16).astype(F32)
            rest = rest - part
            parts[first + k : first + k + 1, :] = part
    parts[ONES : ONES + 3, :] = jnp.ones((3, flat.shape[1]), F32)


def rows_kernel(geom, expand, out, seen, flat, parts, wide):
    tiles = geom.shape[0] // 16
    wide[...] = geom[...].astype(F32)
    for r in range(tiles):
        flat[:, r * TILE : (r + 1) * TILE] = wide[16 * r : 16 * r + 8, :]
    for k in range(seen.shape[0]):
        seen[k] = wide[pl.ds(8 + k, tiles, stride=16), :].astype(BF16)
    write_parts(flat[...], parts)
    for r in range(tiles):
        turned = parts[:, r * TILE : (r + 1) * TILE].T.astype(BF16)
        for q in range(3):
            left = jnp.dot(turned, expand[q], preferred_element_type=F32)
            if q == 1:
                lane = lax.broadcasted_iota(jnp.int32, left.shape, 1)
                left = jnp.where(lane == MASK + r, 1.0, left)
            out[q, r * TILE : (r + 1) * TILE, :] = left.astype(BF16)


def make_rows(geom, expand, tile_blocks):
    tiles = geom.shape[0] // 16
    return pl.pallas_call(
        rows_kernel,
        out_shape=(
            jax.ShapeDtypeStruct((3, tiles * TILE, SLOTS), BF16),
            jax.ShapeDtypeStruct((tile_blocks, tiles, TILE), BF16),
        ),
        scratch_shapes=[
            pltpu.VMEM((8, tiles * TILE), F32),
            pltpu.VMEM((128, tiles * TILE), F32),
            pltpu.VMEM(geom.shape, F32),
        ],
        compiler_params=params(),
    )(geom, expand)


def place():
    blk, quad = lax.axis_index("blk"), lax.axis_index("quad")
    return quad % 4, (quad // 4) * 2 + (blk // 2) % 2, blk // 4, blk % 2


def cols_kernel(dys, *refs):
    groups = refs[: len(dys)]
    seen, out, weights, flat, parts = refs[len(dys) :]
    x, y, z, core = place()
    tiles = len(dys) * 4 * TILES
    column = lax.broadcasted_iota(jnp.int32, (TILE, TILE), 1)
    shard = column // TILES
    there_y = (y + dys[0]) % 4
    for n, dy in enumerate(dys[1:], 1):
        there_y = jnp.where(shard // 4 == n, (y + dy) % 4, there_y)
    there_x = (x + shard) % 4
    blk = (z * 2 + there_y % 2) * 2 + core
    tile = blk * 32 + ((there_y // 2) * 4 + there_x) * TILES + column % TILES
    tile = jnp.where(column < tiles, tile, -1)
    index = lax.broadcasted_iota(jnp.int32, (TILE, TILE), 0)
    pair = jnp.zeros((seen.shape[1], TILE), F32)
    for k in range(seen.shape[0]):
        pick = jnp.where(index + k * TILE == tile, 1.0, 0.0).astype(BF16)
        pair = pair + jnp.dot(seen[k], pick, preferred_element_type=F32)
    for n, group in enumerate(groups):
        for s in range(4):
            weights[(4 * n + s) * SUB : (4 * n + s + 1) * SUB, :] = group[s * MSG : s * MSG + SUB, :]
            for t in range(TILES):
                row = s * MSG + SUB + 16 * t
                j = (4 * n + s) * TILES + t
                flat[:, j * TILE : (j + 1) * TILE] = group[row : row + 16, :].astype(F32)[:8, :]
    write_parts(flat[...], parts)
    pair = pair.astype(BF16)
    for s in range(tiles // 4):
        span = slice(s * SUB, (s + 1) * SUB)
        j = lax.broadcasted_iota(jnp.int32, (TILE, SUB), 0)
        c = lax.broadcasted_iota(jnp.int32, (TILE, SUB), 1)
        spread = jnp.where(j == s * TILES + c // TILE, 1.0, 0.0).astype(BF16)
        open_ = jnp.dot(pair, spread, preferred_element_type=F32)
        out[:MASK, span] = parts[:, span].astype(BF16)
        out[MASK:, span] = ((open_ - 1.0) * 64.0).astype(BF16)


def make_cols(groups, dys, seen):
    cols = len(dys) * 4 * SUB
    return pl.pallas_call(
        functools.partial(cols_kernel, dys),
        out_shape=(
            jax.ShapeDtypeStruct((SLOTS, cols), BF16),
            jax.ShapeDtypeStruct((cols, CASES), BF16),
        ),
        scratch_shapes=[pltpu.VMEM((8, cols), F32), pltpu.VMEM((PARTS, cols), F32)],
        compiler_params=params(),
    )(*groups, seen)


def sweep_kernel(first, has_total, *refs):
    left, right, weights = refs[:3]
    total = refs[3] if has_total else None
    out, terms = refs[-2:]
    chunks = right.shape[1] // CHUNK
    steps = out.shape[0] // ROWS * chunks
    out[...] = total[...] if has_total else jnp.zeros_like(out)

    def generate(step, slot):
        base = step // chunks * ROWS
        col = step % chunks * CHUNK
        for c0 in range(0, CHUNK, 256):
            there = right[:, pl.ds(pl.multiple_of(col + c0, 256), 256)]
            for r0 in range(0, ROWS, 128):
                here = pl.ds(pl.multiple_of(first + base + r0, 128), 128)
                den, face_row, face_col = (
                    jnp.dot(left[q, here, :], there, preferred_element_type=F32) for q in range(3)
                )
                inv = pltpu.reciprocal(den, approx=True)
                term = (jnp.maximum(face_row, 0.0) * inv) * (jnp.maximum(face_col, 0.0) * inv)
                terms[slot, r0 : r0 + 128, c0 : c0 + 256] = term.astype(BF16)

    def gather(step, slot):
        base = pl.multiple_of(step // chunks * ROWS, ROWS)
        col = pl.multiple_of(step % chunks * CHUNK, CHUNK)
        out[pl.ds(base, ROWS), :] += jnp.dot(
            terms[slot], weights[pl.ds(col, CHUNK), :], preferred_element_type=F32
        )

    generate(0, 0)

    def body(i, carry):
        step = i * 2
        gather(step, 0)
        generate(step + 1, 1)
        gather(step + 1, 1)
        generate(jnp.minimum(step + 2, steps - 1), 0)
        return carry

    lax.fori_loop(0, steps // 2, body, 0)


def sweep(left, right, weights, total, first, rows):
    has_total = total is not None
    cols = right.shape[1]
    return pl.pallas_call(
        functools.partial(sweep_kernel, first, has_total),
        out_shape=jax.ShapeDtypeStruct((rows, CASES), F32),
        scratch_shapes=[pltpu.VMEM((2, ROWS, CHUNK), BF16)],
        compiler_params=params(),
        cost_estimate=pl.CostEstimate(
            flops=2 * rows * cols * 1024, bytes_accessed=1 << 20, transcendentals=rows * cols
        ),
    )(left, right, weights, *([total] if has_total else []))


def linear(x, y, z, core):
    return ((z * 2 + y % 2) * 2 + core) * 8 + (y // 2) * 4 + x


def shift(value, dx=0, dy=0, dz=0, dc=0):
    pairs = [
        (linear(x, y, z, c), linear((x + dx) % 4, (y + dy) % 4, (z + dz) % 4, (c + dc) % 2))
        for x in range(4)
        for y in range(4)
        for z in range(4)
        for c in range(2)
    ]
    return lax.ppermute(value, AXES, pairs)


def shards(positions, normals, patch_area, reflect, emission, radiosity, visible):
    lhs = jnp.asarray(expansions(), BF16)
    message, geom = make_message(positions, normals, patch_area[None, :], radiosity, visible)
    line = jnp.stack([geom] + [shift(geom, dz=-d) for d in (1, 2, 3)])
    other = shift(line, dc=1)
    row_geom = jnp.stack([line, other], 1).reshape(8 * GEOM, TILE)
    near = jnp.concatenate([message] + [shift(message, dx=-d) for d in (1, 2, 3)])
    far = {d: shift(near, dy=-d) for d in (1, 3, 2)}
    left, seen = make_rows(row_geom, lhs, visible.shape[1] // TILE)
    right, weights = make_cols([near], [0], seen)
    total = sweep(left, right, weights, None, 0, 8 * SUB)
    right, weights = make_cols([far[1]], [1], seen)
    total = sweep(left, right, weights, total, 0, 8 * SUB)
    right, weights = make_cols([far[3], far[2]], [3, 2], seen)
    sums = []
    for d in (2, 1, 3, 0):
        part = sweep(left, right, weights, total[d * 2 * SUB : (d + 1) * 2 * SUB], d * 2 * SUB, 2 * SUB)
        part = part[:SUB] + shift(part[SUB:], dc=1)
        sums.append(shift(part, dz=d) if d else part)
    irradiation = (sums[0] + sums[1]) + (sums[2] + sums[3])
    return emission + (reflect * (1.0 / math.pi))[:, None] * irradiation


def solution(mesh):
    in_specs = (
        P(None, AXES),
        P(None, AXES),
        P(AXES),
        P(AXES),
        P(AXES, None),
        P(AXES, None),
        P("blk", None),
    )
    return jax.shard_map(
        shards, mesh=mesh, in_specs=in_specs, out_specs=P(AXES, None), check_vma=False
    )
```

time: 805 us -> 162 us (0.20)
  other arithmetic: 319 us -> 1.68 us
  matrix products: 242 us -> 0 us
  Pallas kernels: 0 us -> 113 us
  local copies, waits for them, and re-layouts: 82.5 us -> 12.3 us
  waiting for transfers between devices: 59.5 us -> 10.2 us
  blocking collectives: 28.6 us -> 0 us
  starting transfers between devices: 47.2 us -> 23.7 us
  between operations: 14 us -> 0.14 us
    convert_element_type x139 -> x0, other arithmetic: 308 us -> none  [the longest x56 253 us: compute(): coupling = shaped.reshape(band_rows, sub_size).astype(jnp.bfloat16)]
    dot_general x128 -> x0, matrix products: 242 us -> none  [the longest x72 221 us: compute(): jnp.dot(coupling, far_weighted, preferred_element_type=jnp.float32)]
    pallas_call x0 -> x11, Pallas kernels: none -> 113 us  [the longest x6 99.8 us: sweep(): pl.pallas_call(functools.partial(sweep_kernel, first, has_total), out_sha...]
    reduce_scatter x1 -> x0, waiting for transfers between devices: 46.6 us -> none  [shards(): lax.psum_scatter(rows_total, 'quad', scatter_dimension=0, tiled=True)]
    slice x144 -> x5, local copies, waits for them, and re-layouts: 52.8 us -> 6.89 us  [the longest x4 3.97 us: shards(): part = part[:SUB] + shift(part[SUB:], dc=1)]
    all_gather x1 -> x0, blocking collectives: 28.6 us -> none  [shards(): lax.all_gather(geometry, 'quad', axis=1, tiled=True)]
    ppermute x23 -> x17, starting transfers between devices: 47.1 us -> 23.7 us  [shift(): return lax.ppermute(value, AXES, pairs)]
    mul x72 -> x0, local copies, waits for them, and re-layouts: 14.7 us -> none  [compute(): kernel.reshape(band_rows // tile_side, tile_side, sub_size // tile_side,...]
  transfers between devices with their start and end apart: 25 -> 17, of which waited for: 4 -> 2; matrix products, arithmetic and copies ran while one was open for 70% -> 5% of each run, Pallas kernels for 0% -> 59%
where the time goes in v1:
time: 162 us; the launch traced here: 161 us
  Pallas kernels  113 us (70%)
  starting transfers between devices  23.7 us (15%)
  local copies, waits for them, and re-layouts  12.3 us (8%)
  waiting for transfers between devices  10.2 us (6%)
  other arithmetic  1.68 us (1%)
    pallas_call x6, Pallas kernels, sweep(): pl.pallas_call(functools.partial(sweep_kernel, first, has_total), out_sha...  99.8 us
    ppermute x17, starting transfers between devices, shift(): return lax.ppermute(value, AXES, pairs)  23.7 us
    ppermute x17, waiting for transfers between devices, shift(): return lax.ppermute(value, AXES, pairs)  10.2 us
    pallas_call x3, Pallas kernels, make_cols(): pl.pallas_call(functools.partial(cols_kernel, dys), out_shape=(jax.ShapeD...  7.77 us
    slice x4, local copies, waits for them, and re-layouts, shards(): part = part[:SUB] + shift(part[SUB:], dc=1)  3.97 us
    pallas_call x1, Pallas kernels, make_rows(): pl.pallas_call(rows_kernel, out_shape=(jax.ShapeDtypeStruct((3, tiles * T...  3.72 us
    unnamed x23, local copies, waits for them, and re-layouts  3.47 us
  transfers between devices with their start and end apart: 17, of which 2 were waited for; matrix products, arithmetic and copies ran while one was open for 5% of the time, Pallas kernels for 59%

profile of v1, /device:TPU:1, one launch (start us, length us, event | category | flops | bytes accessed | tf_op | source)
XLA Modules:
  0.0 161.0 jit_solution(18238267849334581549)
XLA Ops:
  0.0 1.3 broadcast_in_dim.4.area
  1.3 1.8 %shard_map.82 = (bf16[576,128]{1,0:T(8,128)(2,1)}, bf16[64,128]{1,0:T(8,128)(2,1)}) custom-call(bf16[3,512]{1,0:T(4,128)(2,1)} %pos.1, bf16[3,512]{1,0:T(4,128)(2,1)} %nrm.1, bf16[1,512]{1,0:T(2,128)(2,1)} %broadcast_in_dim.4.area, f32[512,128]{1,0:T(8,128)} %rad.1, s32[32,512]{1,0:T(8,128)} %vis.1), custom_call_target="tpu_custom_call" | custom-call | tf_op jit(solution)/shard_map/pallas_call | solution.py:71
  3.0 4.6 %collective-permute-start = (bf16[64,128]{1,0:T(8,128)(2,1)}, bf16[64,128]{1,0:T(8,128)(2,1)S(1)}, u32[]{:S(2)}, u32[]{:S(2)}) collective-permute-start(bf16[64,128]{1,0:T(8,128)(2,1)} %get-tuple-element.15), channel_id=1, source_target_pairs={{0,96},{8,104},{32,0},{40,8},{64,32},{72,40},{96,64},{104,72},{16,... | collective-permute-start | bytes 49160 | tf_op jit(solution)/shard_map/ppermute | solution.py:256
  7.6 0.0 collective-permute-start.1
  7.6 0.7 collective-permute-start.2
  8.3 2.5 %collective-permute-start.4 = (bf16[576,128]{1,0:T(8,128)(2,1)}, bf16[576,128]{1,0:T(8,128)(2,1)S(1)}, u32[]{:S(2)}, u32[]{:S(2)}) collective-permute-start(bf16[576,128]{1,0:T(8,128)(2,1)} %get-tuple-element.17), channel_id=1, source_target_pairs={{0,3},{8,11},{32,35},{40,43},{64,67},{72,75},{96,99},{104,107},{16... | collective-permute-start | bytes 442376 | tf_op jit(solution)/shard_map/ppermute | solution.py:256
  10.8 0.5 collective-permute-start.5
  11.3 0.0 collective-permute-done
  11.3 0.6 collective-permute-start.6
  11.9 0.0 collective-permute-done.1
  11.9 0.0 collective-permute-done.2
  11.9 0.7 fusion.4
  12.7 2.4 %collective-permute-start.3 = (bf16[4,64,128]{2,1,0:T(8,128)(2,1)S(1)}, bf16[4,64,128]{2,1,0:T(8,128)(2,1)S(1)}, u32[]{:S(2)}, u32[]{:S(2)}) collective-permute-start(bf16[4,64,128]{2,1,0:T(8,128)(2,1)S(1)} %get-tuple-element.30), channel_id=1, source_target_pairs={{0,8},{8,0},{32,40},{40,32},{64,72},{72,64},{96,104},{104,96},{16,... | collective-permute-start | bytes 196616 | tf_op jit(solution)/shard_map/ppermute | solution.py:256
  15.1 0.9 constant_dynamic-update-slice_fusion.3
  16.0 0.0 collective-permute-done.3
  16.1 0.7 copy.9
  16.7 3.7 %shard_map.83 = (bf16[3,4096,64]{2,1,0:T(8,128)(2,1)}, bf16[4,32,128]{2,1,0:T(8,128)(2,1)}) custom-call(bf16[512,128]{1,0:T(8,128)(2,1)} %bitcast.8, bf16[3,128,64]{2,1,0:T(8,128)(2,1)} %constant.4.clone.expand), custom_call_target="tpu_custom_call" | custom-call | tf_op jit(solution)/shard_map/pallas_call | solution.py:117
  20.4 0.0 collective-permute-done.4
  20.5 0.0 collective-permute-done.5
  20.5 0.0 collective-permute-done.6
  20.6 0.0 copy-start
  20.6 2.8 %collective-permute-start.9 = (bf16[2304,128]{1,0:T(8,128)(2,1)S(1)}, bf16[2304,128]{1,0:T(8,128)(2,1)S(1)}, u32[]{:S(2)}, u32[]{:S(2)}) collective-permute-start(bf16[2304,128]{1,0:T(8,128)(2,1)S(1)} %constant_dynamic-update-slice_fusion.refs_0_), channel_id=1, source_target_pairs={{0,20},{8,28},{32,52},{40,60},{64,84},{72,92},{96,116},{104,124},{... | collective-permute-start | bytes 1769480 | tf_op jit(solution)/shard_map/ppermute | solution.py:256
  23.4 0.0 collective-permute-start.7
  23.4 1.6 %collective-permute-start.8 = (bf16[2304,128]{1,0:T(8,128)(2,1)S(1)}, bf16[2304,128]{1,0:T(8,128)(2,1)S(1)}, u32[]{:S(2)}, u32[]{:S(2)}) collective-permute-start(bf16[2304,128]{1,0:T(8,128)(2,1)S(1)} %constant_dynamic-update-slice_fusion.refs_0_), channel_id=1, source_target_pairs={{0,4},{8,12},{32,36},{40,44},{64,68},{72,76},{96,100},{104,108},{1... | collective-permute-start | bytes 1769480 | tf_op jit(solution)/shard_map/ppermute | solution.py:256
  25.0 0.0 copy-done
  25.0 2.4 %shard_map.86 = (bf16[64,2048]{1,0:T(8,128)(2,1)}, bf16[2048,128]{1,0:T(8,128)(2,1)}) custom-call(bf16[2304,128]{1,0:T(8,128)(2,1)} %copy-done, bf16[4,32,128]{2,1,0:T(8,128)(2,1)} %get-tuple-element.18.refs_2_.refs_1_), custom_call_target="tpu_custom_call" | custom-call | tf_op jit(solution)/shard_map/pallas_call | solution.py:177
  27.4 22.9 %shard_map.87.refs_3_ = f32[4096,128]{1,0:T(8,128)} custom-call(bf16[3,4096,64]{2,1,0:T(8,128)(2,1)} %get-tuple-element.16.refs_0_, bf16[64,2048]{1,0:T(8,128)(2,1)} %get-tuple-element.23.refs_1_, bf16[2048,128]{1,0:T(8,128)(2,1)} %get-tuple-element.24.refs_2_), custom_call_target="tpu_custom_call" | custom-call | flops 17179869184 | bytes 1048576 | tf_op jit(solution)/shard_map/pallas_call | solution.py:233
  50.3 0.0 collective-permute-done.9.refs_0_
  50.3 0.8 copy-done.3
  51.1 2.4 %shard_map.85 = (bf16[64,2048]{1,0:T(8,128)(2,1)}, bf16[2048,128]{1,0:T(8,128)(2,1)}) custom-call(bf16[2304,128]{1,0:T(8,128)(2,1)} %copy-done.3, bf16[4,32,128]{2,1,0:T(8,128)(2,1)} %get-tuple-element.18.refs_2_.refs_1_), custom_call_target="tpu_custom_call" | custom-call | tf_op jit(solution)/shard_map/pallas_call | solution.py:177
  53.5 23.7 %shard_map.88 = f32[4096,128]{1,0:T(8,128)} custom-call(bf16[3,4096,64]{2,1,0:T(8,128)(2,1)} %get-tuple-element.16.refs_0_, bf16[64,2048]{1,0:T(8,128)(2,1)} %get-tuple-element.21.refs_1_, bf16[2048,128]{1,0:T(8,128)(2,1)} %get-tuple-element.22.refs_2_, f32[4096,128]{1,0:T(8,128)} %shard_map.87.refs_3_), custom_call_target="tpu_custom_call" | custom-call | flops 17179869184 | bytes 1048576 | tf_op jit(solution)/shard_map/pallas_call | solution.py:233
  77.1 2.9 %fusion.5 = (f32[1024,128]{1,0:T(8,128)}, f32[1024,128]{1,0:T(8,128)}, f32[1024,128]{1,0:T(8,128)}, f32[1024,128]{1,0:T(8,128)}) fusion(f32[4096,128]{1,0:T(8,128)} %shard_map.88), kind=kLoop, calls=%fused_computation.16 | loop fusion | bytes 4194304 | tf_op jit(solution)/shard_map/slice | solution.py:275
  80.1 0.0 collective-permute-done.7.refs_0_
  80.1 0.0 collective-permute-done.8.refs_1_
  80.1 0.8 copy-done.1
  80.9 0.8 copy-done.2
  81.7 3.1 %shard_map.84 = (bf16[64,4096]{1,0:T(8,128)(2,1)}, bf16[4096,128]{1,0:T(8,128)(2,1)}) custom-call(bf16[2304,128]{1,0:T(8,128)(2,1)} %copy-done.1, bf16[2304,128]{1,0:T(8,128)(2,1)} %copy-done.2, bf16[4,32,128]{2,1,0:T(8,128)(2,1)} %get-tuple-element.18.refs_2_.refs_1_), custom_call_target="tpu_custom_call" | custom-call | tf_op jit(solution)/shard_map/pallas_call | solution.py:177
  84.8 13.3 %shard_map.90 = f32[1024,128]{1,0:T(8,128)} custom-call(bf16[3,4096,64]{2,1,0:T(8,128)(2,1)} %get-tuple-element.16.refs_0_, bf16[64,4096]{1,0:T(8,128)(2,1)} %get-tuple-element.19.refs_1_, bf16[4096,128]{1,0:T(8,128)(2,1)} %get-tuple-element.20.refs_2_, f32[1024,128]{1,0:T(8,128)} %get-tuple-element.25.refs_3_), custom_call_target="tpu_custom_call" | custom-call | flops 8589934592 | bytes 1048576 | tf_op jit(solution)/shard_map/pallas_call | solution.py:233
  98.0 1.0 slice.53
  99.0 2.6 %collective-permute-start.12 = (f32[512,128]{1,0:T(8,128)S(1)}, f32[512,128]{1,0:T(8,128)S(1)}, u32[]{:S(2)}, u32[]{:S(2)}) collective-permute-start(f32[512,128]{1,0:T(8,128)S(1)} %slice.53), channel_id=1, source_target_pairs={{0,8},{8,0},{32,40},{40,32},{64,72},{72,64},{96,104},{104,96},{16,... | collective-permute-start | bytes 786440 | tf_op jit(solution)/shard_map/ppermute | solution.py:256
  101.6 13.3 %shard_map.89 = f32[1024,128]{1,0:T(8,128)} custom-call(bf16[3,4096,64]{2,1,0:T(8,128)(2,1)} %get-tuple-element.16.refs_0_, bf16[64,4096]{1,0:T(8,128)(2,1)} %get-tuple-element.19.refs_1_, bf16[4096,128]{1,0:T(8,128)(2,1)} %get-tuple-element.20.refs_2_, f32[1024,128]{1,0:T(8,128)} %get-tuple-element.28.refs_3_), custom_call_target="tpu_custom_call" | custom-call | flops 8589934592 | bytes 1048576 | tf_op jit(solution)/shard_map/pallas_call | solution.py:233
  114.9 1.0 slice.50
  115.8 0.1 collective-permute-start.10
  115.9 13.3 %shard_map.92 = f32[1024,128]{1,0:T(8,128)} custom-call(bf16[3,4096,64]{2,1,0:T(8,128)(2,1)} %get-tuple-element.16.refs_0_, bf16[64,4096]{1,0:T(8,128)(2,1)} %get-tuple-element.19.refs_1_, bf16[4096,128]{1,0:T(8,128)(2,1)} %get-tuple-element.20.refs_2_, f32[1024,128]{1,0:T(8,128)} %get-tuple-element.26.refs_3_), custom_call_target="tpu_custom_call" | custom-call | flops 8589934592 | bytes 1048576 | tf_op jit(solution)/shard_map/pallas_call | solution.py:233
  129.2 1.0 slice.59
  130.2 0.6 collective-permute-start.16
  130.7 13.4 %shard_map.91 = f32[1024,128]{1,0:T(8,128)} custom-call(bf16[3,4096,64]{2,1,0:T(8,128)(2,1)} %get-tuple-element.16.refs_0_, bf16[64,4096]{1,0:T(8,128)(2,1)} %get-tuple-element.19.refs_1_, bf16[4096,128]{1,0:T(8,128)(2,1)} %get-tuple-element.20.refs_2_, f32[1024,128]{1,0:T(8,128)} %get-tuple-element.27.refs_3_), custom_call_target="tpu_custom_call" | custom-call | flops 8589934592 | bytes 1048576 | tf_op jit(solution)/shard_map/pallas_call | solution.py:233
  144.1 1.1 slice.56
  145.2 0.1 collective-permute-start.14
  145.3 0.0 collective-permute-done.12
  145.3 0.0 copy-done.5
  145.4 2.0 %collective-permute-start.13 = (f32[512,128]{1,0:T(8,128)S(1)}, f32[512,128]{1,0:T(8,128)S(1)}, u32[]{:S(2)}, u32[]{:S(2)}) collective-permute-start(f32[512,128]{1,0:T(8,128)S(1)} %slice_add_fusion.2), channel_id=1, source_target_pairs={{0,32},{8,40},{32,64},{40,72},{64,96},{72,104},{96,0},{104,8},{16,... | collective-permute-start | bytes 786440 | tf_op jit(solution)/shard_map/ppermute | solution.py:256
  147.4 0.0 collective-permute-done.10
  147.4 0.0 copy-done.4
  147.4 1.3 collective-permute-start.11
  148.7 0.0 collective-permute-done.14
  148.7 0.0 copy-done.6
  148.7 1.3 collective-permute-start.15
  150.0 0.0 copy-done.9
  150.0 0.0 collective-permute-done.16
  150.0 4.0 %collective-permute-done.13 = f32[512,128]{1,0:T(8,128)S(1)} collective-permute-done((f32[512,128]{1,0:T(8,128)S(1)}, f32[512,128]{1,0:T(8,128)S(1)}, u32[]{:S(2)}, u32[]{:S(2)}) %collective-permute-start.13) | collective-permute-done | bytes 262176 | tf_op jit(solution)/shard_map/ppermute | solution.py:256
  154.0 6.1 %collective-permute-done.11 = f32[512,128]{1,0:T(8,128)S(1)} collective-permute-done((f32[512,128]{1,0:T(8,128)S(1)}, f32[512,128]{1,0:T(8,128)S(1)}, u32[]{:S(2)}, u32[]{:S(2)}) %collective-permute-start.11) | collective-permute-done | bytes 262176 | tf_op jit(solution)/shard_map/ppermute | solution.py:256
  160.1 0.0 collective-permute-done.15
  160.2 0.8 fusion.3
  (19 shorter events, 0.2 us)
Async XLA Ops:
  3.0 8.3 %collective-permute-start = (bf16[64,128]{1,0:T(8,128)(2,1)}, bf16[64,128]{1,0:T(8,128)(2,1)S(1)}, u32[]{:S(2)}, u32[]{:S(2)}) collective-permute-start(bf16[64,128]{1,0:T(8,128)(2,1)} %get-tuple-element.15), channel_id=1, source_target_pairs={{0,96},{8,104},{32,0},{40,8},{64,32},{72,40},{96,64},{104,72},{16,... | collective-permute-start | bytes 49160 | tf_op jit(solution)/shard_map/ppermute | solution.py:256
  7.6 4.3 %collective-permute-start.1 = (bf16[64,128]{1,0:T(8,128)(2,1)}, bf16[64,128]{1,0:T(8,128)(2,1)S(1)}, u32[]{:S(2)}, u32[]{:S(2)}) collective-permute-start(bf16[64,128]{1,0:T(8,128)(2,1)} %get-tuple-element.15), channel_id=1, source_target_pairs={{0,64},{8,72},{32,96},{40,104},{64,0},{72,8},{96,32},{104,40},{16,... | collective-permute-start | bytes 49160 | tf_op jit(solution)/shard_map/ppermute | solution.py:256
  7.6 4.3 %collective-permute-start.2 = (bf16[64,128]{1,0:T(8,128)(2,1)}, bf16[64,128]{1,0:T(8,128)(2,1)S(1)}, u32[]{:S(2)}, u32[]{:S(2)}) collective-permute-start(bf16[64,128]{1,0:T(8,128)(2,1)} %get-tuple-element.15), channel_id=1, source_target_pairs={{0,32},{8,40},{32,64},{40,72},{64,96},{72,104},{96,0},{104,8},{16,... | collective-permute-start | bytes 49160 | tf_op jit(solution)/shard_map/ppermute | solution.py:256
  8.3 12.1 %collective-permute-start.4 = (bf16[576,128]{1,0:T(8,128)(2,1)}, bf16[576,128]{1,0:T(8,128)(2,1)S(1)}, u32[]{:S(2)}, u32[]{:S(2)}) collective-permute-start(bf16[576,128]{1,0:T(8,128)(2,1)} %get-tuple-element.17), channel_id=1, source_target_pairs={{0,3},{8,11},{32,35},{40,43},{64,67},{72,75},{96,99},{104,107},{16... | collective-permute-start | bytes 442376 | tf_op jit(solution)/shard_map/ppermute | solution.py:256
  10.8 9.7 %collective-permute-start.5 = (bf16[576,128]{1,0:T(8,128)(2,1)}, bf16[576,128]{1,0:T(8,128)(2,1)S(1)}, u32[]{:S(2)}, u32[]{:S(2)}) collective-permute-start(bf16[576,128]{1,0:T(8,128)(2,1)} %get-tuple-element.17), channel_id=1, source_target_pairs={{0,2},{8,10},{32,34},{40,42},{64,66},{72,74},{96,98},{104,106},{16... | collective-permute-start | bytes 442376 | tf_op jit(solution)/shard_map/ppermute | solution.py:256
  11.3 9.2 %collective-permute-start.6 = (bf16[576,128]{1,0:T(8,128)(2,1)}, bf16[576,128]{1,0:T(8,128)(2,1)S(1)}, u32[]{:S(2)}, u32[]{:S(2)}) collective-permute-start(bf16[576,128]{1,0:T(8,128)(2,1)} %get-tuple-element.17), channel_id=1, source_target_pairs={{0,1},{8,9},{32,33},{40,41},{64,65},{72,73},{96,97},{104,105},{16,... | collective-permute-start | bytes 442376 | tf_op jit(solution)/shard_map/ppermute | solution.py:256
  12.7 3.4 %collective-permute-start.3 = (bf16[4,64,128]{2,1,0:T(8,128)(2,1)S(1)}, bf16[4,64,128]{2,1,0:T(8,128)(2,1)S(1)}, u32[]{:S(2)}, u32[]{:S(2)}) collective-permute-start(bf16[4,64,128]{2,1,0:T(8,128)(2,1)S(1)} %get-tuple-element.30), channel_id=1, source_target_pairs={{0,8},{8,0},{32,40},{40,32},{64,72},{72,64},{96,104},{104,96},{16,... | collective-permute-start | bytes 196616 | tf_op jit(solution)/shard_map/ppermute | solution.py:256
  20.6 4.5 %copy-start = (bf16[2304,128]{1,0:T(8,128)(2,1)}, bf16[2304,128]{1,0:T(8,128)(2,1)S(1)}, u32[]{:S(2)}) copy-start(bf16[2304,128]{1,0:T(8,128)(2,1)S(1)} %constant_dynamic-update-slice_fusion.refs_0_) | copy-start | bytes 1769476
  20.6 29.7 %collective-permute-start.9 = (bf16[2304,128]{1,0:T(8,128)(2,1)S(1)}, bf16[2304,128]{1,0:T(8,128)(2,1)S(1)}, u32[]{:S(2)}, u32[]{:S(2)}) collective-permute-start(bf16[2304,128]{1,0:T(8,128)(2,1)S(1)} %constant_dynamic-update-slice_fusion.refs_0_), channel_id=1, source_target_pairs={{0,20},{8,28},{32,52},{40,60},{64,84},{72,92},{96,116},{104,124},{... | collective-permute-start | bytes 1769480 | tf_op jit(solution)/shard_map/ppermute | solution.py:256
  23.4 56.7 %collective-permute-start.7 = (bf16[2304,128]{1,0:T(8,128)(2,1)S(1)}, bf16[2304,128]{1,0:T(8,128)(2,1)S(1)}, u32[]{:S(2)}, u32[]{:S(2)}) collective-permute-start(bf16[2304,128]{1,0:T(8,128)(2,1)S(1)} %constant_dynamic-update-slice_fusion.refs_0_), channel_id=1, source_target_pairs={{0,16},{8,24},{32,48},{40,56},{64,80},{72,88},{96,112},{104,120},{... | collective-permute-start | bytes 1769480 | tf_op jit(solution)/shard_map/ppermute | solution.py:256
  23.4 56.7 %collective-permute-start.8 = (bf16[2304,128]{1,0:T(8,128)(2,1)S(1)}, bf16[2304,128]{1,0:T(8,128)(2,1)S(1)}, u32[]{:S(2)}, u32[]{:S(2)}) collective-permute-start(bf16[2304,128]{1,0:T(8,128)(2,1)S(1)} %constant_dynamic-update-slice_fusion.refs_0_), channel_id=1, source_target_pairs={{0,4},{8,12},{32,36},{40,44},{64,68},{72,76},{96,100},{104,108},{1... | collective-permute-start | bytes 1769480 | tf_op jit(solution)/shard_map/ppermute | solution.py:256
  50.3 0.8 copy-start.3
  80.1 0.8 copy-start.1
  80.9 0.8 copy-start.2
  99.0 46.3 %collective-permute-start.12 = (f32[512,128]{1,0:T(8,128)S(1)}, f32[512,128]{1,0:T(8,128)S(1)}, u32[]{:S(2)}, u32[]{:S(2)}) collective-permute-start(f32[512,128]{1,0:T(8,128)S(1)} %slice.53), channel_id=1, source_target_pairs={{0,8},{8,0},{32,40},{40,32},{64,72},{72,64},{96,104},{104,96},{16,... | collective-permute-start | bytes 786440 | tf_op jit(solution)/shard_map/ppermute | solution.py:256
  115.8 31.5 %collective-permute-start.10 = (f32[512,128]{1,0:T(8,128)S(1)}, f32[512,128]{1,0:T(8,128)S(1)}, u32[]{:S(2)}, u32[]{:S(2)}) collective-permute-start(f32[512,128]{1,0:T(8,128)S(1)} %slice.50), channel_id=1, source_target_pairs={{0,8},{8,0},{32,40},{40,32},{64,72},{72,64},{96,104},{104,96},{16,... | collective-permute-start | bytes 786440 | tf_op jit(solution)/shard_map/ppermute | solution.py:256
  130.2 19.9 %collective-permute-start.16 = (f32[512,128]{1,0:T(8,128)S(1)}, f32[512,128]{1,0:T(8,128)S(1)}, u32[]{:S(2)}, u32[]{:S(2)}) collective-permute-start(f32[512,128]{1,0:T(8,128)S(1)} %slice.59), channel_id=1, source_target_pairs={{0,8},{8,0},{32,40},{40,32},{64,72},{72,64},{96,104},{104,96},{16,... | collective-permute-start | bytes 786440 | tf_op jit(solution)/shard_map/ppermute | solution.py:256
  130.7 14.6 %copy-start.5 = (f32[1024,128]{1,0:T(8,128)S(1)}, f32[1024,128]{1,0:T(8,128)}, u32[]{:S(2)}) copy-start(f32[1024,128]{1,0:T(8,128)} %shard_map.90) | copy-start | bytes 1572868
  130.7 16.6 %copy-start.4 = (f32[1024,128]{1,0:T(8,128)S(1)}, f32[1024,128]{1,0:T(8,128)}, u32[]{:S(2)}) copy-start(f32[1024,128]{1,0:T(8,128)} %shard_map.89) | copy-start | bytes 1572868
  144.1 4.6 %copy-start.6 = (f32[1024,128]{1,0:T(8,128)S(1)}, f32[1024,128]{1,0:T(8,128)}, u32[]{:S(2)}) copy-start(f32[1024,128]{1,0:T(8,128)} %shard_map.91) | copy-start | bytes 1572868
  144.1 5.9 %copy-start.9 = (f32[512]{0:T(512)S(1)}, f32[512]{0:T(512)}, u32[]{:S(2)}) copy-start(f32[512]{0:T(512)} %param.11) | copy-start | bytes 6148
  144.1 16.0 %copy-start.7 = (f32[1024,128]{1,0:T(8,128)S(1)}, f32[1024,128]{1,0:T(8,128)}, u32[]{:S(2)}) copy-start(f32[1024,128]{1,0:T(8,128)} %shard_map.92) | copy-start | bytes 1572868
  144.1 16.0 %copy-start.8 = (f32[512,128]{1,0:T(8,128)S(1)}, f32[512,128]{1,0:T(8,128)}, u32[]{:S(2)}) copy-start(f32[512,128]{1,0:T(8,128)} %param.12) | copy-start | bytes 786436
  145.2 3.5 %collective-permute-start.14 = (f32[512,128]{1,0:T(8,128)S(1)}, f32[512,128]{1,0:T(8,128)S(1)}, u32[]{:S(2)}, u32[]{:S(2)}) collective-permute-start(f32[512,128]{1,0:T(8,128)S(1)} %slice.56), channel_id=1, source_target_pairs={{0,8},{8,0},{32,40},{40,32},{64,72},{72,64},{96,104},{104,96},{16,... | collective-permute-start | bytes 786440 | tf_op jit(solution)/shard_map/ppermute | solution.py:256
  145.4 8.7 %collective-permute-start.13 = (f32[512,128]{1,0:T(8,128)S(1)}, f32[512,128]{1,0:T(8,128)S(1)}, u32[]{:S(2)}, u32[]{:S(2)}) collective-permute-start(f32[512,128]{1,0:T(8,128)S(1)} %slice_add_fusion.2), channel_id=1, source_target_pairs={{0,32},{8,40},{32,64},{40,72},{64,96},{72,104},{96,0},{104,8},{16,... | collective-permute-start | bytes 786440 | tf_op jit(solution)/shard_map/ppermute | solution.py:256
  147.4 12.7 %collective-permute-start.11 = (f32[512,128]{1,0:T(8,128)S(1)}, f32[512,128]{1,0:T(8,128)S(1)}, u32[]{:S(2)}, u32[]{:S(2)}) collective-permute-start(f32[512,128]{1,0:T(8,128)S(1)} %slice_add_fusion.3), channel_id=1, source_target_pairs={{0,64},{8,72},{32,96},{40,104},{64,0},{72,8},{96,32},{104,40},{16,... | collective-permute-start | bytes 786440 | tf_op jit(solution)/shard_map/ppermute | solution.py:256
  148.7 11.4 %collective-permute-start.15 = (f32[512,128]{1,0:T(8,128)S(1)}, f32[512,128]{1,0:T(8,128)S(1)}, u32[]{:S(2)}, u32[]{:S(2)}) collective-permute-start(f32[512,128]{1,0:T(8,128)S(1)} %slice_add_fusion.1), channel_id=1, source_target_pairs={{0,96},{8,104},{32,0},{40,8},{64,32},{72,40},{96,64},{104,72},{16,... | collective-permute-start | bytes 786440 | tf_op jit(solution)/shard_map/ppermute | solution.py:256

commit v2 on v1

--- a/solution.py
+++ b/solution.py
@@ -187,17 +187,18 @@
 
 def sweep_kernel(first, has_total, *refs):
     left, right, weights = refs[:3]
-    total = refs[3] if has_total else None
     out, terms = refs[-2:]
     chunks = right.shape[1] // CHUNK
-    steps = out.shape[0] // ROWS * chunks
-    out[...] = total[...] if has_total else jnp.zeros_like(out)
+    count = out.shape[0]
+    steps = count // ROWS * chunks
+    out[...] = refs[3][first : first + count, :] if has_total else jnp.zeros_like(out)
 
     def generate(step, slot):
         base = step // chunks * ROWS
         col = step % chunks * CHUNK
         for c0 in range(0, CHUNK, 256):
-            there = right[:, pl.ds(pl.multiple_of(col + c0, 256), 256)]
+            cols = pl.ds(pl.multiple_of(col + c0, 256), 256)
+            there = right[:, cols]
             for r0 in range(0, ROWS, 128):
                 here = pl.ds(pl.multiple_of(first + base + r0, 128), 128)
                 den, face_row, face_col = (
@@ -221,24 +222,27 @@
         gather(step, 0)
         generate(step + 1, 1)
         gather(step + 1, 1)
-        generate(jnp.minimum(step + 2, steps - 1), 0)
+        generate(step + 2, 0)
         return carry
 
-    lax.fori_loop(0, steps // 2, body, 0)
-
-
-def sweep(left, right, weights, total, first, rows):
+    lax.fori_loop(0, steps // 2 - 1, body, 0)
+    gather(steps - 2, 0)
+    generate(steps - 1, 1)
+    gather(steps - 1, 1)
+
+
+def sweep(left, cols, total, first, count):
     has_total = total is not None
-    cols = right.shape[1]
+    width = cols[0].shape[1]
     return pl.pallas_call(
         functools.partial(sweep_kernel, first, has_total),
-        out_shape=jax.ShapeDtypeStruct((rows, CASES), F32),
+        out_shape=jax.ShapeDtypeStruct((count, CASES), F32),
         scratch_shapes=[pltpu.VMEM((2, ROWS, CHUNK), BF16)],
         compiler_params=params(),
         cost_estimate=pl.CostEstimate(
-            flops=2 * rows * cols * 1024, bytes_accessed=1 << 20, transcendentals=rows * cols
-        ),
-    )(left, right, weights, *([total] if has_total else []))
+            flops=2 * count * width * 1536, bytes_accessed=1 << 20, transcendentals=count * width
+        ),
+    )(left, *cols, *([total] if has_total else []))
 
 
 def linear(x, y, z, core):
@@ -265,17 +269,16 @@
     near = jnp.concatenate([message] + [shift(message, dx=-d) for d in (1, 2, 3)])
     far = {d: shift(near, dy=-d) for d in (1, 3, 2)}
     left, seen = make_rows(row_geom, lhs, visible.shape[1] // TILE)
-    right, weights = make_cols([near], [0], seen)
-    total = sweep(left, right, weights, None, 0, 8 * SUB)
-    right, weights = make_cols([far[1]], [1], seen)
-    total = sweep(left, right, weights, total, 0, 8 * SUB)
-    right, weights = make_cols([far[3], far[2]], [3, 2], seen)
-    sums = []
-    for d in (2, 1, 3, 0):
-        part = sweep(left, right, weights, total[d * 2 * SUB : (d + 1) * 2 * SUB], d * 2 * SUB, 2 * SUB)
-        part = part[:SUB] + shift(part[SUB:], dc=1)
-        sums.append(shift(part, dz=d) if d else part)
-    irradiation = (sums[0] + sums[1]) + (sums[2] + sums[3])
+    total = sweep(left, make_cols([near], [0], seen), None, 0, 8 * SUB)
+    total = sweep(left, make_cols([far[1]], [1], seen), total, 0, 8 * SUB)
+    cols = make_cols([far[3], far[2]], [3, 2], seen)
+    part = sweep(left, cols, total, 2 * SUB, 6 * SUB).reshape(3, 2, SUB, CASES)
+    away = part[:, 0] + shift(part[:, 1], dc=1)
+    away, cols = lax.optimization_barrier((away, cols))
+    sent = [shift(away[d - 1], dz=d) for d in (2, 1, 3)]
+    part = sweep(left, cols, total, 0, 2 * SUB)
+    own = part[:SUB] + shift(part[SUB:], dc=1)
+    irradiation = own + (sent[0] + sent[1] + sent[2])
     return emission + (reflect * (1.0 / math.pi))[:, None] * irradiation
 
 

time: 162 us -> 144 us (0.89)
  waiting for transfers between devices: 10.2 us -> 3.08 us
  Pallas kernels: 113 us -> 106 us
  local copies, waits for them, and re-layouts: 12.3 us -> 7.72 us
    pallas_call x6 -> x4, Pallas kernels: 99.8 us -> 92.6 us  [sweep(): pl.pallas_call(functools.partial(sweep_kernel, first, has_total), out_sha...]
    ppermute x17 -> x15, waiting for transfers between devices: 10.2 us -> 3.08 us  [shift(): return lax.ppermute(value, AXES, pairs)]
    slice x5 -> x1, local copies, waits for them, and re-layouts: 6.89 us -> 0.97 us  [shards(): own = part[:SUB] + shift(part[SUB:], dc=1)]
    ppermute x17 -> x15, starting transfers between devices: 23.7 us -> 24.4 us  [shift(): return lax.ppermute(value, AXES, pairs)]
    unnamed x23 -> x17, local copies, waits for them, and re-layouts: 3.47 us -> 3.46 us
  transfers between devices with their start and end apart: 17 -> 15, of which waited for: 2 -> 2; matrix products, arithmetic and copies ran while one was open for 5% -> 2% of each run, Pallas kernels for 59% -> 47%
where the time goes in v2:
time: 144 us
  Pallas kernels  106 us (74%)
  starting transfers between devices  24.4 us (17%)
  local copies, waits for them, and re-layouts  7.72 us (5%)
  waiting for transfers between devices  3.08 us (2%)
  other arithmetic  2.62 us (2%)
    pallas_call x4, Pallas kernels, sweep(): pl.pallas_call(functools.partial(sweep_kernel, first, has_total), out_sha...  92.6 us
    ppermute x15, starting transfers between devices, shift(): return lax.ppermute(value, AXES, pairs)  24.4 us
    pallas_call x3, Pallas kernels, make_cols(): pl.pallas_call(functools.partial(cols_kernel, dys), out_shape=(jax.ShapeD...  7.85 us
    pallas_call x1, Pallas kernels, make_rows(): pl.pallas_call(rows_kernel, out_shape=(jax.ShapeDtypeStruct((3, tiles * T...  3.73 us
    unnamed x17, local copies, waits for them, and re-layouts  3.46 us
    ppermute x15, waiting for transfers between devices, shift(): return lax.ppermute(value, AXES, pairs)  3.08 us
  transfers between devices with their start and end apart: 15, of which 2 were waited for; matrix products, arithmetic and copies ran while one was open for 2% of the time, Pallas kernels for 47%

profile of v2, /device:TPU:1, one launch (start us, length us, event | category | flops | bytes accessed | tf_op | source)
XLA Modules:
  0.0 144.0 jit_solution(15002585427099692587)
XLA Ops:
  0.0 1.3 broadcast_in_dim.4.area
  1.3 1.8 %shard_map.82 = (bf16[576,128]{1,0:T(8,128)(2,1)}, bf16[64,128]{1,0:T(8,128)(2,1)}) custom-call(bf16[3,512]{1,0:T(4,128)(2,1)} %pos.1, bf16[3,512]{1,0:T(4,128)(2,1)} %nrm.1, bf16[1,512]{1,0:T(2,128)(2,1)} %broadcast_in_dim.4.area, f32[512,128]{1,0:T(8,128)} %rad.1, s32[32,512]{1,0:T(8,128)} %vis.1), custom_call_target="tpu_custom_call" | custom-call | tf_op jit(solution)/shard_map/pallas_call | solution.py:71
  3.0 4.6 %collective-permute-start = (bf16[64,128]{1,0:T(8,128)(2,1)}, bf16[64,128]{1,0:T(8,128)(2,1)S(1)}, u32[]{:S(2)}, u32[]{:S(2)}) collective-permute-start(bf16[64,128]{1,0:T(8,128)(2,1)} %get-tuple-element.18), channel_id=1, source_target_pairs={{0,96},{8,104},{32,0},{40,8},{64,32},{72,40},{96,64},{104,72},{16,... | collective-permute-start | bytes 49160 | tf_op jit(solution)/shard_map/ppermute | solution.py:260
  7.6 0.0 collective-permute-start.1
  7.6 0.7 collective-permute-start.2
  8.3 2.5 %collective-permute-start.4 = (bf16[576,128]{1,0:T(8,128)(2,1)}, bf16[576,128]{1,0:T(8,128)(2,1)S(1)}, u32[]{:S(2)}, u32[]{:S(2)}) collective-permute-start(bf16[576,128]{1,0:T(8,128)(2,1)} %get-tuple-element.20), channel_id=1, source_target_pairs={{0,3},{8,11},{32,35},{40,43},{64,67},{72,75},{96,99},{104,107},{16... | collective-permute-start | bytes 442376 | tf_op jit(solution)/shard_map/ppermute | solution.py:260
  10.8 0.5 collective-permute-start.5
  11.3 0.0 collective-permute-done
  11.3 0.6 collective-permute-start.6
  11.9 0.0 collective-permute-done.1
  11.9 0.0 collective-permute-done.2
  12.0 0.7 fusion.4
  12.7 2.4 %collective-permute-start.3 = (bf16[4,64,128]{2,1,0:T(8,128)(2,1)S(1)}, bf16[4,64,128]{2,1,0:T(8,128)(2,1)S(1)}, u32[]{:S(2)}, u32[]{:S(2)}) collective-permute-start(bf16[4,64,128]{2,1,0:T(8,128)(2,1)S(1)} %get-tuple-element.35), channel_id=1, source_target_pairs={{0,8},{8,0},{32,40},{40,32},{64,72},{72,64},{96,104},{104,96},{16,... | collective-permute-start | bytes 196616 | tf_op jit(solution)/shard_map/ppermute | solution.py:260
  15.1 0.9 constant_dynamic-update-slice_fusion.3
  16.0 0.0 collective-permute-done.3
  16.1 0.7 copy.10
  16.7 3.7 %shard_map.83 = (bf16[3,4096,64]{2,1,0:T(8,128)(2,1)}, bf16[4,32,128]{2,1,0:T(8,128)(2,1)}) custom-call(bf16[512,128]{1,0:T(8,128)(2,1)} %bitcast.27, bf16[3,128,64]{2,1,0:T(8,128)(2,1)} %constant.4.clone.expand), custom_call_target="tpu_custom_call" | custom-call | tf_op jit(solution)/shard_map/pallas_call | solution.py:117
  20.5 0.0 collective-permute-done.4
  20.5 0.0 collective-permute-done.5
  20.5 0.0 collective-permute-done.6
  20.6 0.0 copy-start.1
  20.6 2.8 %collective-permute-start.9 = (bf16[2304,128]{1,0:T(8,128)(2,1)S(1)}, bf16[2304,128]{1,0:T(8,128)(2,1)S(1)}, u32[]{:S(2)}, u32[]{:S(2)}) collective-permute-start(bf16[2304,128]{1,0:T(8,128)(2,1)S(1)} %constant_dynamic-update-slice_fusion.refs_0_), channel_id=1, source_target_pairs={{0,20},{8,28},{32,52},{40,60},{64,84},{72,92},{96,116},{104,124},{... | collective-permute-start | bytes 1769480 | tf_op jit(solution)/shard_map/ppermute | solution.py:260
  23.4 0.0 collective-permute-start.7
  23.4 1.6 %collective-permute-start.8 = (bf16[2304,128]{1,0:T(8,128)(2,1)S(1)}, bf16[2304,128]{1,0:T(8,128)(2,1)S(1)}, u32[]{:S(2)}, u32[]{:S(2)}) collective-permute-start(bf16[2304,128]{1,0:T(8,128)(2,1)S(1)} %constant_dynamic-update-slice_fusion.refs_0_), channel_id=1, source_target_pairs={{0,4},{8,12},{32,36},{40,44},{64,68},{72,76},{96,100},{104,108},{1... | collective-permute-start | bytes 1769480 | tf_op jit(solution)/shard_map/ppermute | solution.py:260
  25.0 0.0 copy-done.1
  25.0 2.4 %shard_map.86 = (bf16[64,2048]{1,0:T(8,128)(2,1)}, bf16[2048,128]{1,0:T(8,128)(2,1)}) custom-call(bf16[2304,128]{1,0:T(8,128)(2,1)} %copy-done.1, bf16[4,32,128]{2,1,0:T(8,128)(2,1)} %get-tuple-element.21.refs_2_.refs_1_), custom_call_target="tpu_custom_call" | custom-call | tf_op jit(solution)/shard_map/pallas_call | solution.py:177
  27.4 22.6 %shard_map.87.refs_3_ = f32[4096,128]{1,0:T(8,128)} custom-call(bf16[3,4096,64]{2,1,0:T(8,128)(2,1)} %get-tuple-element.19.refs_0_, bf16[64,2048]{1,0:T(8,128)(2,1)} %get-tuple-element.26.refs_1_, bf16[2048,128]{1,0:T(8,128)(2,1)} %get-tuple-element.27.refs_2_), custom_call_target="tpu_custom_call" | custom-call | flops 25769803776 | bytes 1048576 | tf_op jit(solution)/shard_map/pallas_call | solution.py:237
  50.0 0.0 collective-permute-done.9.refs_0_
  50.0 0.0 copy-start.4
  50.0 0.8 copy-done.4
  50.8 2.4 %shard_map.85 = (bf16[64,2048]{1,0:T(8,128)(2,1)}, bf16[2048,128]{1,0:T(8,128)(2,1)}) custom-call(bf16[2304,128]{1,0:T(8,128)(2,1)} %copy-done.4, bf16[4,32,128]{2,1,0:T(8,128)(2,1)} %get-tuple-element.21.refs_2_.refs_1_), custom_call_target="tpu_custom_call" | custom-call | tf_op jit(solution)/shard_map/pallas_call | solution.py:177
  53.1 23.4 %shard_map.88.refs_3_ = f32[4096,128]{1,0:T(8,128)} custom-call(bf16[3,4096,64]{2,1,0:T(8,128)(2,1)} %get-tuple-element.19.refs_0_, bf16[64,2048]{1,0:T(8,128)(2,1)} %get-tuple-element.24.refs_1_, bf16[2048,128]{1,0:T(8,128)(2,1)} %get-tuple-element.25.refs_2_, f32[4096,128]{1,0:T(8,128)} %shard_map.87.refs_3_), custom_call_target="tpu_custom_call" | custom-call | flops 25769803776 | bytes 1048576 | tf_op jit(solution)/shard_map/pallas_call | solution.py:237
  76.6 0.0 collective-permute-done.7.refs_0_
  76.6 0.0 copy-start.2
  76.6 0.0 collective-permute-done.8.refs_1_
  76.6 0.8 copy-done.2
  77.4 0.0 copy-start.3
  77.4 0.8 copy-done.3
  78.2 3.1 %shard_map.84 = (bf16[64,4096]{1,0:T(8,128)(2,1)}, bf16[4096,128]{1,0:T(8,128)(2,1)}) custom-call(bf16[2304,128]{1,0:T(8,128)(2,1)} %copy-done.2, bf16[2304,128]{1,0:T(8,128)(2,1)} %copy-done.3, bf16[4,32,128]{2,1,0:T(8,128)(2,1)} %get-tuple-element.21.refs_2_.refs_1_), custom_call_target="tpu_custom_call" | custom-call | tf_op jit(solution)/shard_map/pallas_call | solution.py:177
  81.4 33.1 %shard_map.89 = f32[3072,128]{1,0:T(8,128)} custom-call(bf16[3,4096,64]{2,1,0:T(8,128)(2,1)} %get-tuple-element.19.refs_0_, bf16[64,4096]{1,0:T(8,128)(2,1)} %get-tuple-element.28.refs_1_, bf16[4096,128]{1,0:T(8,128)(2,1)} %get-tuple-element.29.refs_2_, f32[4096,128]{1,0:T(8,128)} %shard_map.88.refs_3_), custom_call_target="tpu_custom_call" | custom-call | flops 38654705664 | bytes 1048576 | tf_op jit(solution)/shard_map/pallas_call | solution.py:237
  114.5 0.0 copy-start
  114.5 1.3 slice_bitcast_fusion
  115.8 2.3 %collective-permute-start.10 = (f32[3,512,128]{2,1,0:T(8,128)S(1)}, f32[3,512,128]{2,1,0:T(8,128)S(1)}, u32[]{:S(2)}, u32[]{:S(2)}) collective-permute-start(f32[3,512,128]{2,1,0:T(8,128)S(1)} %slice_bitcast_fusion), channel_id=1, source_target_pairs={{0,8},{8,0},{32,40},{40,32},{64,72},{72,64},{96,104},{104,96},{16,... | collective-permute-start | bytes 2359304 | tf_op jit(solution)/shard_map/ppermute | solution.py:260
  118.1 1.9 %collective-permute-done.10 = f32[3,512,128]{2,1,0:T(8,128)S(1)} collective-permute-done((f32[3,512,128]{2,1,0:T(8,128)S(1)}, f32[3,512,128]{2,1,0:T(8,128)S(1)}, u32[]{:S(2)}, u32[]{:S(2)}) %collective-permute-start.10) | collective-permute-done | bytes 786464 | tf_op jit(solution)/shard_map/ppermute | solution.py:260
  120.0 0.0 copy-done
  120.0 0.1 fusion
  120.1 0.1 slice_bitcast_fusion.3
  120.1 2.3 %collective-permute-start.12 = (f32[512,128]{1,0:T(8,128)S(1)}, f32[512,128]{1,0:T(8,128)S(1)}, u32[]{:S(2)}, u32[]{:S(2)}) collective-permute-start(f32[512,128]{1,0:T(8,128)S(1)} %get-tuple-element.33), channel_id=1, source_target_pairs={{0,64},{8,72},{32,96},{40,104},{64,0},{72,8},{96,32},{104,40},{16,... | collective-permute-start | bytes 786440 | tf_op jit(solution)/shard_map/ppermute | solution.py:260
  122.5 0.3 collective-permute-start.13
  122.8 0.0 copy-start.6
  122.8 0.0 copy-start.5
  122.8 2.4 %collective-permute-start.14 = (f32[512,128]{1,0:T(8,128)S(1)}, f32[512,128]{1,0:T(8,128)S(1)}, u32[]{:S(2)}, u32[]{:S(2)}) collective-permute-start(f32[512,128]{1,0:T(8,128)S(1)} %get-tuple-element.32), channel_id=1, source_target_pairs={{0,96},{8,104},{32,0},{40,8},{64,32},{72,40},{96,64},{104,72},{16,... | collective-permute-start | bytes 786440 | tf_op jit(solution)/shard_map/ppermute | solution.py:260
  125.2 13.6 %shard_map.90 = f32[1024,128]{1,0:T(8,128)} custom-call(bf16[3,4096,64]{2,1,0:T(8,128)(2,1)} %get-tuple-element.19.refs_0_, bf16[64,4096]{1,0:T(8,128)(2,1)} %get-tuple-element.28.refs_1_, bf16[4096,128]{1,0:T(8,128)(2,1)} %get-tuple-element.29.refs_2_, f32[4096,128]{1,0:T(8,128)} %shard_map.88.refs_3_), custom_call_target="tpu_custom_call" | custom-call | flops 12884901888 | bytes 1048576 | tf_op jit(solution)/shard_map/pallas_call | solution.py:237
  138.7 1.0 slice.31
  139.7 1.3 collective-permute-start.11
  141.0 0.0 copy-done.6
  141.0 0.0 collective-permute-done.12
  141.0 0.0 collective-permute-done.13
  141.0 0.0 collective-permute-done.14
  141.0 1.1 collective-permute-done.11
  142.2 0.0 copy-done.5
  142.2 1.8 %fusion.3 = f32[512,128]{1,0:T(8,128)} fusion(f32[512,128]{1,0:T(8,128)S(1)} %copy-done.5, f32[512,128]{1,0:T(8,128)S(1)} %collective-permute-done.11, f32[1024,128]{1,0:T(8,128)} %shard_map.90, f32[512,128]{1,0:T(8,128)S(1)} %collective-permute-done.14, f32[512,128]{1,0:T(8,128)S(1)} %collective-permute-done.12, f32[512,128]{1,0:T(8,128)S(1)} %collective-permute-done.13, ...), kind=kLoop, calls=%fused_computation.6 | loop fusion | flops 393216 | bytes 1837056 | tf_op jit(solution)/shard_map/add | solution.py:282
  (5 shorter events, 0.1 us)
Async XLA Ops:
  3.0 8.3 %collective-permute-start = (bf16[64,128]{1,0:T(8,128)(2,1)}, bf16[64,128]{1,0:T(8,128)(2,1)S(1)}, u32[]{:S(2)}, u32[]{:S(2)}) collective-permute-start(bf16[64,128]{1,0:T(8,128)(2,1)} %get-tuple-element.18), channel_id=1, source_target_pairs={{0,96},{8,104},{32,0},{40,8},{64,32},{72,40},{96,64},{104,72},{16,... | collective-permute-start | bytes 49160 | tf_op jit(solution)/shard_map/ppermute | solution.py:260
  7.6 4.3 %collective-permute-start.1 = (bf16[64,128]{1,0:T(8,128)(2,1)}, bf16[64,128]{1,0:T(8,128)(2,1)S(1)}, u32[]{:S(2)}, u32[]{:S(2)}) collective-permute-start(bf16[64,128]{1,0:T(8,128)(2,1)} %get-tuple-element.18), channel_id=1, source_target_pairs={{0,64},{8,72},{32,96},{40,104},{64,0},{72,8},{96,32},{104,40},{16,... | collective-permute-start | bytes 49160 | tf_op jit(solution)/shard_map/ppermute | solution.py:260
  7.6 4.3 %collective-permute-start.2 = (bf16[64,128]{1,0:T(8,128)(2,1)}, bf16[64,128]{1,0:T(8,128)(2,1)S(1)}, u32[]{:S(2)}, u32[]{:S(2)}) collective-permute-start(bf16[64,128]{1,0:T(8,128)(2,1)} %get-tuple-element.18), channel_id=1, source_target_pairs={{0,32},{8,40},{32,64},{40,72},{64,96},{72,104},{96,0},{104,8},{16,... | collective-permute-start | bytes 49160 | tf_op jit(solution)/shard_map/ppermute | solution.py:260
  8.3 12.1 %collective-permute-start.4 = (bf16[576,128]{1,0:T(8,128)(2,1)}, bf16[576,128]{1,0:T(8,128)(2,1)S(1)}, u32[]{:S(2)}, u32[]{:S(2)}) collective-permute-start(bf16[576,128]{1,0:T(8,128)(2,1)} %get-tuple-element.20), channel_id=1, source_target_pairs={{0,3},{8,11},{32,35},{40,43},{64,67},{72,75},{96,99},{104,107},{16... | collective-permute-start | bytes 442376 | tf_op jit(solution)/shard_map/ppermute | solution.py:260
  10.8 9.7 %collective-permute-start.5 = (bf16[576,128]{1,0:T(8,128)(2,1)}, bf16[576,128]{1,0:T(8,128)(2,1)S(1)}, u32[]{:S(2)}, u32[]{:S(2)}) collective-permute-start(bf16[576,128]{1,0:T(8,128)(2,1)} %get-tuple-element.20), channel_id=1, source_target_pairs={{0,2},{8,10},{32,34},{40,42},{64,66},{72,74},{96,98},{104,106},{16... | collective-permute-start | bytes 442376 | tf_op jit(solution)/shard_map/ppermute | solution.py:260
  11.3 9.2 %collective-permute-start.6 = (bf16[576,128]{1,0:T(8,128)(2,1)}, bf16[576,128]{1,0:T(8,128)(2,1)S(1)}, u32[]{:S(2)}, u32[]{:S(2)}) collective-permute-start(bf16[576,128]{1,0:T(8,128)(2,1)} %get-tuple-element.20), channel_id=1, source_target_pairs={{0,1},{8,9},{32,33},{40,41},{64,65},{72,73},{96,97},{104,105},{16,... | collective-permute-start | bytes 442376 | tf_op jit(solution)/shard_map/ppermute | solution.py:260
  12.7 3.4 %collective-permute-start.3 = (bf16[4,64,128]{2,1,0:T(8,128)(2,1)S(1)}, bf16[4,64,128]{2,1,0:T(8,128)(2,1)S(1)}, u32[]{:S(2)}, u32[]{:S(2)}) collective-permute-start(bf16[4,64,128]{2,1,0:T(8,128)(2,1)S(1)} %get-tuple-element.35), channel_id=1, source_target_pairs={{0,8},{8,0},{32,40},{40,32},{64,72},{72,64},{96,104},{104,96},{16,... | collective-permute-start | bytes 196616 | tf_op jit(solution)/shard_map/ppermute | solution.py:260
  20.6 4.5 %copy-start.1 = (bf16[2304,128]{1,0:T(8,128)(2,1)}, bf16[2304,128]{1,0:T(8,128)(2,1)S(1)}, u32[]{:S(2)}) copy-start(bf16[2304,128]{1,0:T(8,128)(2,1)S(1)} %constant_dynamic-update-slice_fusion.refs_0_) | copy-start | bytes 1769476
  20.6 29.4 %collective-permute-start.9 = (bf16[2304,128]{1,0:T(8,128)(2,1)S(1)}, bf16[2304,128]{1,0:T(8,128)(2,1)S(1)}, u32[]{:S(2)}, u32[]{:S(2)}) collective-permute-start(bf16[2304,128]{1,0:T(8,128)(2,1)S(1)} %constant_dynamic-update-slice_fusion.refs_0_), channel_id=1, source_target_pairs={{0,20},{8,28},{32,52},{40,60},{64,84},{72,92},{96,116},{104,124},{... | collective-permute-start | bytes 1769480 | tf_op jit(solution)/shard_map/ppermute | solution.py:260
  23.4 53.2 %collective-permute-start.7 = (bf16[2304,128]{1,0:T(8,128)(2,1)S(1)}, bf16[2304,128]{1,0:T(8,128)(2,1)S(1)}, u32[]{:S(2)}, u32[]{:S(2)}) collective-permute-start(bf16[2304,128]{1,0:T(8,128)(2,1)S(1)} %constant_dynamic-update-slice_fusion.refs_0_), channel_id=1, source_target_pairs={{0,16},{8,24},{32,48},{40,56},{64,80},{72,88},{96,112},{104,120},{... | collective-permute-start | bytes 1769480 | tf_op jit(solution)/shard_map/ppermute | solution.py:260
  23.4 53.2 %collective-permute-start.8 = (bf16[2304,128]{1,0:T(8,128)(2,1)S(1)}, bf16[2304,128]{1,0:T(8,128)(2,1)S(1)}, u32[]{:S(2)}, u32[]{:S(2)}) collective-permute-start(bf16[2304,128]{1,0:T(8,128)(2,1)S(1)} %constant_dynamic-update-slice_fusion.refs_0_), channel_id=1, source_target_pairs={{0,4},{8,12},{32,36},{40,44},{64,68},{72,76},{96,100},{104,108},{1... | collective-permute-start | bytes 1769480 | tf_op jit(solution)/shard_map/ppermute | solution.py:260
  50.0 0.8 copy-start.4
  76.6 0.8 copy-start.2
  77.4 0.8 copy-start.3
  114.5 5.6 %copy-start = (f32[3072,128]{1,0:T(8,128)S(1)}, f32[3072,128]{1,0:T(8,128)}, u32[]{:S(2)}) copy-start(f32[3072,128]{1,0:T(8,128)} %shard_map.89) | copy-start | bytes 4718596
  115.8 4.2 %collective-permute-start.10 = (f32[3,512,128]{2,1,0:T(8,128)S(1)}, f32[3,512,128]{2,1,0:T(8,128)S(1)}, u32[]{:S(2)}, u32[]{:S(2)}) collective-permute-start(f32[3,512,128]{2,1,0:T(8,128)S(1)} %slice_bitcast_fusion), channel_id=1, source_target_pairs={{0,8},{8,0},{32,40},{40,32},{64,72},{72,64},{96,104},{104,96},{16,... | collective-permute-start | bytes 2359304 | tf_op jit(solution)/shard_map/ppermute | solution.py:260
  120.1 20.9 %collective-permute-start.12 = (f32[512,128]{1,0:T(8,128)S(1)}, f32[512,128]{1,0:T(8,128)S(1)}, u32[]{:S(2)}, u32[]{:S(2)}) collective-permute-start(f32[512,128]{1,0:T(8,128)S(1)} %get-tuple-element.33), channel_id=1, source_target_pairs={{0,64},{8,72},{32,96},{40,104},{64,0},{72,8},{96,32},{104,40},{16,... | collective-permute-start | bytes 786440 | tf_op jit(solution)/shard_map/ppermute | solution.py:260
  122.5 18.5 %collective-permute-start.13 = (f32[512,128]{1,0:T(8,128)S(1)}, f32[512,128]{1,0:T(8,128)S(1)}, u32[]{:S(2)}, u32[]{:S(2)}) collective-permute-start(f32[512,128]{1,0:T(8,128)S(1)} %get-tuple-element.31), channel_id=1, source_target_pairs={{0,32},{8,40},{32,64},{40,72},{64,96},{72,104},{96,0},{104,8},{16,... | collective-permute-start | bytes 786440 | tf_op jit(solution)/shard_map/ppermute | solution.py:260
  122.8 18.2 %copy-start.6 = (f32[512]{0:T(512)S(1)}, f32[512]{0:T(512)}, u32[]{:S(2)}) copy-start(f32[512]{0:T(512)} %param.11) | copy-start | bytes 6148
  122.8 19.4 %copy-start.5 = (f32[512,128]{1,0:T(8,128)S(1)}, f32[512,128]{1,0:T(8,128)}, u32[]{:S(2)}) copy-start(f32[512,128]{1,0:T(8,128)} %param.12) | copy-start | bytes 786436
  122.8 18.3 %collective-permute-start.14 = (f32[512,128]{1,0:T(8,128)S(1)}, f32[512,128]{1,0:T(8,128)S(1)}, u32[]{:S(2)}, u32[]{:S(2)}) collective-permute-start(f32[512,128]{1,0:T(8,128)S(1)} %get-tuple-element.32), channel_id=1, source_target_pairs={{0,96},{8,104},{32,0},{40,8},{64,32},{72,40},{96,64},{104,72},{16,... | collective-permute-start | bytes 786440 | tf_op jit(solution)/shard_map/ppermute | solution.py:260
  139.7 2.5 %collective-permute-start.11 = (f32[512,128]{1,0:T(8,128)S(1)}, f32[512,128]{1,0:T(8,128)S(1)}, u32[]{:S(2)}, u32[]{:S(2)}) collective-permute-start(f32[512,128]{1,0:T(8,128)S(1)} %slice.31), channel_id=1, source_target_pairs={{0,8},{8,0},{32,40},{40,32},{64,72},{72,64},{96,104},{104,96},{16,... | collective-permute-start | bytes 786440 | tf_op jit(solution)/shard_map/ppermute | solution.py:260

commit v3 on v2

--- a/solution.py
+++ b/solution.py
@@ -20,7 +20,7 @@
 MSG = SUB + GEOM
 SLOTS = 64
 MASK = 32
-CHUNK = 512
+CHUNK = 1024
 ROWS = 1024
 VMEM = 56 << 20
 
@@ -185,9 +185,12 @@
     )(*groups, seen)
 
 
-def sweep_kernel(first, has_total, *refs):
+def sweep_kernel(first, has_total, split, *refs):
     left, right, weights = refs[:3]
-    out, terms = refs[-2:]
+    if split:
+        near, far, terms, out = refs[-4:]
+    else:
+        out, terms = refs[-2:]
     chunks = right.shape[1] // CHUNK
     count = out.shape[0]
     steps = count // ROWS * chunks
@@ -229,15 +232,23 @@
     gather(steps - 2, 0)
     generate(steps - 1, 1)
     gather(steps - 1, 1)
-
-
-def sweep(left, cols, total, first, count):
+    if split:
+        for n in range(count // (2 * SUB)):
+            here = slice(n * SUB, (n + 1) * SUB)
+            near[here, :] = out[2 * n * SUB : (2 * n + 1) * SUB, :]
+            far[here, :] = out[(2 * n + 1) * SUB : (2 * n + 2) * SUB, :]
+
+
+def sweep(left, cols, total, first, count, split=False):
     has_total = total is not None
     width = cols[0].shape[1]
+    shape = jax.ShapeDtypeStruct((count, CASES), F32)
+    half = jax.ShapeDtypeStruct((count // 2, CASES), F32)
     return pl.pallas_call(
-        functools.partial(sweep_kernel, first, has_total),
-        out_shape=jax.ShapeDtypeStruct((count, CASES), F32),
-        scratch_shapes=[pltpu.VMEM((2, ROWS, CHUNK), BF16)],
+        functools.partial(sweep_kernel, first, has_total, split),
+        out_shape=(half, half) if split else shape,
+        scratch_shapes=[pltpu.VMEM((2, ROWS, CHUNK), BF16)]
+        + ([pltpu.VMEM((count, CASES), F32)] if split else []),
         compiler_params=params(),
         cost_estimate=pl.CostEstimate(
             flops=2 * count * width * 1536, bytes_accessed=1 << 20, transcendentals=count * width
@@ -270,14 +281,13 @@
     far = {d: shift(near, dy=-d) for d in (1, 3, 2)}
     left, seen = make_rows(row_geom, lhs, visible.shape[1] // TILE)
     total = sweep(left, make_cols([near], [0], seen), None, 0, 8 * SUB)
-    total = sweep(left, make_cols([far[1]], [1], seen), total, 0, 8 * SUB)
-    cols = make_cols([far[3], far[2]], [3, 2], seen)
-    part = sweep(left, cols, total, 2 * SUB, 6 * SUB).reshape(3, 2, SUB, CASES)
-    away = part[:, 0] + shift(part[:, 1], dc=1)
+    cols = make_cols([far[1], far[3], far[2]], [1, 3, 2], seen)
+    mine, others = sweep(left, cols, total, 2 * SUB, 6 * SUB, True)
+    away = mine + shift(others, dc=1)
     away, cols = lax.optimization_barrier((away, cols))
-    sent = [shift(away[d - 1], dz=d) for d in (2, 1, 3)]
-    part = sweep(left, cols, total, 0, 2 * SUB)
-    own = part[:SUB] + shift(part[SUB:], dc=1)
+    sent = [shift(away[(d - 1) * SUB : d * SUB], dz=d) for d in (2, 1, 3)]
+    mine, others = sweep(left, cols, total, 0, 2 * SUB, True)
+    own = mine + shift(others, dc=1)
     irradiation = own + (sent[0] + sent[1] + sent[2])
     return emission + (reflect * (1.0 / math.pi))[:, None] * irradiation
 

time: 144 us -> 134 us (0.931)
  Pallas kernels: 106 us -> 97.8 us
  local copies, waits for them, and re-layouts: 7.72 us -> 4.86 us
    pallas_call x4 -> x3, Pallas kernels: 92.6 us -> 86.2 us  [sweep(): pl.pallas_call(functools.partial(sweep_kernel, first, has_total, split),...]
    pallas_call x3 -> x2, Pallas kernels: 7.85 us -> 6.09 us  [make_cols(): pl.pallas_call(functools.partial(cols_kernel, dys), out_shape=(jax.ShapeD...]
    unnamed x17 -> x15, local copies, waits for them, and re-layouts: 3.46 us -> 2.87 us
  transfers between devices with their start and end apart: 15 -> 15, of which waited for: 2 -> 2; matrix products, arithmetic and copies ran while one was open for 2% -> 2% of each run, Pallas kernels for 47% -> 35%
where the time goes in v3:
time: 134 us
  Pallas kernels  97.8 us (73%)
  starting transfers between devices  23.8 us (18%)
  local copies, waits for them, and re-layouts  4.86 us (4%)
  other arithmetic  3.75 us (3%)
  waiting for transfers between devices  3.5 us (3%)
    pallas_call x3, Pallas kernels, sweep(): pl.pallas_call(functools.partial(sweep_kernel, first, has_total, split),...  86.2 us
    ppermute x15, starting transfers between devices, shift(): return lax.ppermute(value, AXES, pairs)  23.8 us
    pallas_call x2, Pallas kernels, make_cols(): pl.pallas_call(functools.partial(cols_kernel, dys), out_shape=(jax.ShapeD...  6.09 us
    pallas_call x1, Pallas kernels, make_rows(): pl.pallas_call(rows_kernel, out_shape=(jax.ShapeDtypeStruct((3, tiles * T...  3.73 us
    ppermute x15, waiting for transfers between devices, shift(): return lax.ppermute(value, AXES, pairs)  3.5 us
    unnamed x15, local copies, waits for them, and re-layouts  2.87 us
  transfers between devices with their start and end apart: 15, of which 2 were waited for; matrix products, arithmetic and copies ran while one was open for 2% of the time, Pallas kernels for 35%

profile of v3, /device:TPU:1, one launch (start us, length us, event | category | flops | bytes accessed | tf_op | source)
XLA Modules:
  0.0 133.9 jit_solution(10180575636808564543)
XLA Ops:
  0.0 1.3 broadcast_in_dim.4.area
  1.3 1.8 %shard_map.82 = (bf16[576,128]{1,0:T(8,128)(2,1)}, bf16[64,128]{1,0:T(8,128)(2,1)}) custom-call(bf16[3,512]{1,0:T(4,128)(2,1)} %pos.1, bf16[3,512]{1,0:T(4,128)(2,1)} %nrm.1, bf16[1,512]{1,0:T(2,128)(2,1)} %broadcast_in_dim.4.area, f32[512,128]{1,0:T(8,128)} %rad.1, s32[32,512]{1,0:T(8,128)} %vis.1), custom_call_target="tpu_custom_call" | custom-call | tf_op jit(solution)/shard_map/pallas_call | solution.py:71
  3.0 2.5 %collective-permute-start.2 = (bf16[64,128]{1,0:T(8,128)(2,1)}, bf16[64,128]{1,0:T(8,128)(2,1)S(1)}, u32[]{:S(2)}, u32[]{:S(2)}) collective-permute-start(bf16[64,128]{1,0:T(8,128)(2,1)} %get-tuple-element.20), channel_id=1, source_target_pairs={{0,32},{8,40},{32,64},{40,72},{64,96},{72,104},{96,0},{104,8},{16,... | collective-permute-start | bytes 49160 | tf_op jit(solution)/shard_map/ppermute | solution.py:271
  5.5 3.3 %collective-permute-start.1 = (bf16[64,128]{1,0:T(8,128)(2,1)}, bf16[64,128]{1,0:T(8,128)(2,1)S(1)}, u32[]{:S(2)}, u32[]{:S(2)}) collective-permute-start(bf16[64,128]{1,0:T(8,128)(2,1)} %get-tuple-element.20), channel_id=1, source_target_pairs={{0,64},{8,72},{32,96},{40,104},{64,0},{72,8},{96,32},{104,40},{16,... | collective-permute-start | bytes 49160 | tf_op jit(solution)/shard_map/ppermute | solution.py:271
  8.8 0.7 collective-permute-start
  9.5 2.5 %collective-permute-start.4 = (bf16[576,128]{1,0:T(8,128)(2,1)}, bf16[576,128]{1,0:T(8,128)(2,1)S(1)}, u32[]{:S(2)}, u32[]{:S(2)}) collective-permute-start(bf16[576,128]{1,0:T(8,128)(2,1)} %get-tuple-element.22), channel_id=1, source_target_pairs={{0,3},{8,11},{32,35},{40,43},{64,67},{72,75},{96,99},{104,107},{16... | collective-permute-start | bytes 442376 | tf_op jit(solution)/shard_map/ppermute | solution.py:271
  12.0 0.5 collective-permute-start.5
  12.5 0.0 collective-permute-done.2
  12.5 0.6 collective-permute-start.6
  13.2 0.0 collective-permute-done.1
  13.2 0.0 collective-permute-done
  13.2 0.7 fusion
  13.9 2.4 %collective-permute-start.3 = (bf16[4,64,128]{2,1,0:T(8,128)(2,1)S(1)}, bf16[4,64,128]{2,1,0:T(8,128)(2,1)S(1)}, u32[]{:S(2)}, u32[]{:S(2)}) collective-permute-start(bf16[4,64,128]{2,1,0:T(8,128)(2,1)S(1)} %get-tuple-element.39), channel_id=1, source_target_pairs={{0,8},{8,0},{32,40},{40,32},{64,72},{72,64},{96,104},{104,96},{16,... | collective-permute-start | bytes 196616 | tf_op jit(solution)/shard_map/ppermute | solution.py:271
  16.3 0.9 constant_dynamic-update-slice_fusion.3
  17.3 0.0 collective-permute-done.3
  17.3 0.7 copy.9
  17.9 3.7 %shard_map.83 = (bf16[3,4096,64]{2,1,0:T(8,128)(2,1)}, bf16[4,32,128]{2,1,0:T(8,128)(2,1)}) custom-call(bf16[512,128]{1,0:T(8,128)(2,1)} %bitcast.8, bf16[3,128,64]{2,1,0:T(8,128)(2,1)} %constant.4.clone.expand), custom_call_target="tpu_custom_call" | custom-call | tf_op jit(solution)/shard_map/pallas_call | solution.py:117
  21.7 0.0 collective-permute-done.4
  21.7 0.0 collective-permute-done.5
  21.7 0.0 collective-permute-done.6
  21.8 0.0 copy-start
  21.8 2.8 %collective-permute-start.7 = (bf16[2304,128]{1,0:T(8,128)(2,1)S(1)}, bf16[2304,128]{1,0:T(8,128)(2,1)S(1)}, u32[]{:S(2)}, u32[]{:S(2)}) collective-permute-start(bf16[2304,128]{1,0:T(8,128)(2,1)S(1)} %constant_dynamic-update-slice_fusion.refs_0_), channel_id=1, source_target_pairs={{0,20},{8,28},{32,52},{40,60},{64,84},{72,92},{96,116},{104,124},{... | collective-permute-start | bytes 1769480 | tf_op jit(solution)/shard_map/ppermute | solution.py:271
  24.6 0.0 collective-permute-start.8
  24.6 1.6 %collective-permute-start.9 = (bf16[2304,128]{1,0:T(8,128)(2,1)S(1)}, bf16[2304,128]{1,0:T(8,128)(2,1)S(1)}, u32[]{:S(2)}, u32[]{:S(2)}) collective-permute-start(bf16[2304,128]{1,0:T(8,128)(2,1)S(1)} %constant_dynamic-update-slice_fusion.refs_0_), channel_id=1, source_target_pairs={{0,4},{8,12},{32,36},{40,44},{64,68},{72,76},{96,100},{104,108},{1... | collective-permute-start | bytes 1769480 | tf_op jit(solution)/shard_map/ppermute | solution.py:271
  26.2 0.0 copy-done
  26.2 2.4 %shard_map.85 = (bf16[64,2048]{1,0:T(8,128)(2,1)}, bf16[2048,128]{1,0:T(8,128)(2,1)}) custom-call(bf16[2304,128]{1,0:T(8,128)(2,1)} %copy-done, bf16[4,32,128]{2,1,0:T(8,128)(2,1)} %get-tuple-element.23.refs_3_.refs_1_), custom_call_target="tpu_custom_call" | custom-call | tf_op jit(solution)/shard_map/pallas_call | solution.py:177
  28.6 22.1 %shard_map.86.refs_3_ = f32[4096,128]{1,0:T(8,128)} custom-call(bf16[3,4096,64]{2,1,0:T(8,128)(2,1)} %get-tuple-element.21.refs_0_, bf16[64,2048]{1,0:T(8,128)(2,1)} %get-tuple-element.26.refs_1_, bf16[2048,128]{1,0:T(8,128)(2,1)} %get-tuple-element.27.refs_2_), custom_call_target="tpu_custom_call" | custom-call | flops 25769803776 | bytes 1048576 | tf_op jit(solution)/shard_map/pallas_call | solution.py:247
  50.7 0.0 collective-permute-done.7.refs_0_
  50.7 0.0 copy-start.1
  50.7 0.0 collective-permute-done.8.refs_1_
  50.7 0.0 copy-start.2
  50.7 0.0 collective-permute-done.9.refs_2_
  50.7 0.9 copy-done.1
  51.6 0.2 copy-done.2
  51.8 0.0 copy-start.3
  51.8 0.8 copy-done.3
  52.6 3.7 %shard_map.84 = (bf16[64,6144]{1,0:T(8,128)(2,1)}, bf16[6144,128]{1,0:T(8,128)(2,1)}) custom-call(bf16[2304,128]{1,0:T(8,128)(2,1)} %copy-done.1, bf16[2304,128]{1,0:T(8,128)(2,1)} %copy-done.2, bf16[2304,128]{1,0:T(8,128)(2,1)} %copy-done.3, bf16[4,32,128]{2,1,0:T(8,128)(2,1)} %get-tuple-element.23.refs_3_.refs_1_), custom_call_target="tpu_custom_call" | custom-call | tf_op jit(solution)/shard_map/pallas_call | solution.py:177
  56.4 45.9 %shard_map.87 = (f32[1536,128]{1,0:T(8,128)}, f32[1536,128]{1,0:T(8,128)}) custom-call(bf16[3,4096,64]{2,1,0:T(8,128)(2,1)} %get-tuple-element.21.refs_0_, bf16[64,6144]{1,0:T(8,128)(2,1)} %get-tuple-element.30.refs_1_, bf16[6144,128]{1,0:T(8,128)(2,1)} %get-tuple-element.31.refs_2_, f32[4096,128]{1,0:T(8,128)} %shard_map.86.refs_3_), custom_call_target="tpu_custom_call" | custom-call | flops 57982058496 | bytes 1048576 | tf_op jit(solution)/shard_map/pallas_call | solution.py:247
  102.3 3.3 %collective-permute-start.10 = (f32[1536,128]{1,0:T(8,128)}, f32[1536,128]{1,0:T(8,128)S(1)}, u32[]{:S(2)}, u32[]{:S(2)}) collective-permute-start(f32[1536,128]{1,0:T(8,128)} %get-tuple-element.29), channel_id=1, source_target_pairs={{0,8},{8,0},{32,40},{40,32},{64,72},{72,64},{96,104},{104,96},{16,... | collective-permute-start | bytes 2359304 | tf_op jit(solution)/shard_map/ppermute | solution.py:271
  105.6 2.1 %collective-permute-done.10 = f32[1536,128]{1,0:T(8,128)S(1)} collective-permute-done((f32[1536,128]{1,0:T(8,128)}, f32[1536,128]{1,0:T(8,128)S(1)}, u32[]{:S(2)}, u32[]{:S(2)}) %collective-permute-start.10) | collective-permute-done | bytes 786464 | tf_op jit(solution)/shard_map/ppermute | solution.py:271
  107.7 1.2 add.18
  108.9 0.1 fusion.1
  109.0 0.5 collective-permute-start.14
  109.5 2.1 %collective-permute-start.12 = (f32[512,128]{1,0:T(8,128)S(1)}, f32[512,128]{1,0:T(8,128)S(1)}, u32[]{:S(2)}, u32[]{:S(2)}) collective-permute-start(f32[512,128]{1,0:T(8,128)S(1)} %get-tuple-element.37), channel_id=1, source_target_pairs={{0,64},{8,72},{32,96},{40,104},{64,0},{72,8},{96,32},{104,40},{16,... | collective-permute-start | bytes 786440 | tf_op jit(solution)/shard_map/ppermute | solution.py:271
  111.6 0.0 copy-start.5
  111.6 0.0 copy-start.4
  111.6 0.0 collective-permute-start.13
  111.6 18.2 %shard_map.88 = (f32[512,128]{1,0:T(8,128)}, f32[512,128]{1,0:T(8,128)}) custom-call(bf16[3,4096,64]{2,1,0:T(8,128)(2,1)} %get-tuple-element.21.refs_0_, bf16[64,6144]{1,0:T(8,128)(2,1)} %get-tuple-element.30.refs_1_, bf16[6144,128]{1,0:T(8,128)(2,1)} %get-tuple-element.31.refs_2_, f32[4096,128]{1,0:T(8,128)} %shard_map.86.refs_3_), custom_call_target="tpu_custom_call" | custom-call | flops 19327352832 | bytes 1048576 | tf_op jit(solution)/shard_map/pallas_call | solution.py:247
  129.8 0.9 collective-permute-start.11
  130.7 0.0 copy-done.5
  130.7 0.0 collective-permute-done.14
  130.7 0.0 collective-permute-done.12
  130.7 0.0 collective-permute-done.13
  130.7 1.3 %collective-permute-done.11 = f32[512,128]{1,0:T(8,128)S(1)} collective-permute-done((f32[512,128]{1,0:T(8,128)}, f32[512,128]{1,0:T(8,128)S(1)}, u32[]{:S(2)}, u32[]{:S(2)}) %collective-permute-start.11) | collective-permute-done | bytes 262176 | tf_op jit(solution)/shard_map/ppermute | solution.py:271
  132.1 0.0 copy-done.4
  132.1 1.8 %multiply_add_fusion = f32[512,128]{1,0:T(8,128)} fusion(f32[512,128]{1,0:T(8,128)S(1)} %copy-done.4, f32[512,128]{1,0:T(8,128)S(1)} %collective-permute-done.14, f32[512,128]{1,0:T(8,128)S(1)} %collective-permute-done.12, f32[512,128]{1,0:T(8,128)S(1)} %collective-permute-done.13, f32[512,128]{1,0:T(8,128)} %get-tuple-element.32, ...), kind=kLoop, calls=%fused_computation | loop fusion | flops 393216 | bytes 1837056 | tf_op jit(solution)/shard_map/add | solution.py:292
  (5 shorter events, 0.1 us)
Async XLA Ops:
  3.0 9.5 %collective-permute-start.2 = (bf16[64,128]{1,0:T(8,128)(2,1)}, bf16[64,128]{1,0:T(8,128)(2,1)S(1)}, u32[]{:S(2)}, u32[]{:S(2)}) collective-permute-start(bf16[64,128]{1,0:T(8,128)(2,1)} %get-tuple-element.20), channel_id=1, source_target_pairs={{0,32},{8,40},{32,64},{40,72},{64,96},{72,104},{96,0},{104,8},{16,... | collective-permute-start | bytes 49160 | tf_op jit(solution)/shard_map/ppermute | solution.py:271
  5.5 7.6 %collective-permute-start.1 = (bf16[64,128]{1,0:T(8,128)(2,1)}, bf16[64,128]{1,0:T(8,128)(2,1)S(1)}, u32[]{:S(2)}, u32[]{:S(2)}) collective-permute-start(bf16[64,128]{1,0:T(8,128)(2,1)} %get-tuple-element.20), channel_id=1, source_target_pairs={{0,64},{8,72},{32,96},{40,104},{64,0},{72,8},{96,32},{104,40},{16,... | collective-permute-start | bytes 49160 | tf_op jit(solution)/shard_map/ppermute | solution.py:271
  8.8 4.3 %collective-permute-start = (bf16[64,128]{1,0:T(8,128)(2,1)}, bf16[64,128]{1,0:T(8,128)(2,1)S(1)}, u32[]{:S(2)}, u32[]{:S(2)}) collective-permute-start(bf16[64,128]{1,0:T(8,128)(2,1)} %get-tuple-element.20), channel_id=1, source_target_pairs={{0,96},{8,104},{32,0},{40,8},{64,32},{72,40},{96,64},{104,72},{16,... | collective-permute-start | bytes 49160 | tf_op jit(solution)/shard_map/ppermute | solution.py:271
  9.5 12.1 %collective-permute-start.4 = (bf16[576,128]{1,0:T(8,128)(2,1)}, bf16[576,128]{1,0:T(8,128)(2,1)S(1)}, u32[]{:S(2)}, u32[]{:S(2)}) collective-permute-start(bf16[576,128]{1,0:T(8,128)(2,1)} %get-tuple-element.22), channel_id=1, source_target_pairs={{0,3},{8,11},{32,35},{40,43},{64,67},{72,75},{96,99},{104,107},{16... | collective-permute-start | bytes 442376 | tf_op jit(solution)/shard_map/ppermute | solution.py:271
  12.0 9.7 %collective-permute-start.5 = (bf16[576,128]{1,0:T(8,128)(2,1)}, bf16[576,128]{1,0:T(8,128)(2,1)S(1)}, u32[]{:S(2)}, u32[]{:S(2)}) collective-permute-start(bf16[576,128]{1,0:T(8,128)(2,1)} %get-tuple-element.22), channel_id=1, source_target_pairs={{0,2},{8,10},{32,34},{40,42},{64,66},{72,74},{96,98},{104,106},{16... | collective-permute-start | bytes 442376 | tf_op jit(solution)/shard_map/ppermute | solution.py:271
  12.5 9.2 %collective-permute-start.6 = (bf16[576,128]{1,0:T(8,128)(2,1)}, bf16[576,128]{1,0:T(8,128)(2,1)S(1)}, u32[]{:S(2)}, u32[]{:S(2)}) collective-permute-start(bf16[576,128]{1,0:T(8,128)(2,1)} %get-tuple-element.22), channel_id=1, source_target_pairs={{0,1},{8,9},{32,33},{40,41},{64,65},{72,73},{96,97},{104,105},{16,... | collective-permute-start | bytes 442376 | tf_op jit(solution)/shard_map/ppermute | solution.py:271
  13.9 3.4 %collective-permute-start.3 = (bf16[4,64,128]{2,1,0:T(8,128)(2,1)S(1)}, bf16[4,64,128]{2,1,0:T(8,128)(2,1)S(1)}, u32[]{:S(2)}, u32[]{:S(2)}) collective-permute-start(bf16[4,64,128]{2,1,0:T(8,128)(2,1)S(1)} %get-tuple-element.39), channel_id=1, source_target_pairs={{0,8},{8,0},{32,40},{40,32},{64,72},{72,64},{96,104},{104,96},{16,... | collective-permute-start | bytes 196616 | tf_op jit(solution)/shard_map/ppermute | solution.py:271
  21.8 4.5 %copy-start = (bf16[2304,128]{1,0:T(8,128)(2,1)}, bf16[2304,128]{1,0:T(8,128)(2,1)S(1)}, u32[]{:S(2)}) copy-start(bf16[2304,128]{1,0:T(8,128)(2,1)S(1)} %constant_dynamic-update-slice_fusion.refs_0_) | copy-start | bytes 1769476
  21.8 28.9 %collective-permute-start.7 = (bf16[2304,128]{1,0:T(8,128)(2,1)S(1)}, bf16[2304,128]{1,0:T(8,128)(2,1)S(1)}, u32[]{:S(2)}, u32[]{:S(2)}) collective-permute-start(bf16[2304,128]{1,0:T(8,128)(2,1)S(1)} %constant_dynamic-update-slice_fusion.refs_0_), channel_id=1, source_target_pairs={{0,20},{8,28},{32,52},{40,60},{64,84},{72,92},{96,116},{104,124},{... | collective-permute-start | bytes 1769480 | tf_op jit(solution)/shard_map/ppermute | solution.py:271
  24.6 26.1 %collective-permute-start.8 = (bf16[2304,128]{1,0:T(8,128)(2,1)S(1)}, bf16[2304,128]{1,0:T(8,128)(2,1)S(1)}, u32[]{:S(2)}, u32[]{:S(2)}) collective-permute-start(bf16[2304,128]{1,0:T(8,128)(2,1)S(1)} %constant_dynamic-update-slice_fusion.refs_0_), channel_id=1, source_target_pairs={{0,16},{8,24},{32,48},{40,56},{64,80},{72,88},{96,112},{104,120},{... | collective-permute-start | bytes 1769480 | tf_op jit(solution)/shard_map/ppermute | solution.py:271
  24.6 26.1 %collective-permute-start.9 = (bf16[2304,128]{1,0:T(8,128)(2,1)S(1)}, bf16[2304,128]{1,0:T(8,128)(2,1)S(1)}, u32[]{:S(2)}, u32[]{:S(2)}) collective-permute-start(bf16[2304,128]{1,0:T(8,128)(2,1)S(1)} %constant_dynamic-update-slice_fusion.refs_0_), channel_id=1, source_target_pairs={{0,4},{8,12},{32,36},{40,44},{64,68},{72,76},{96,100},{104,108},{1... | collective-permute-start | bytes 1769480 | tf_op jit(solution)/shard_map/ppermute | solution.py:271
  50.7 0.9 copy-start.1
  50.7 1.1 copy-start.2
  51.8 0.8 copy-start.3
  102.3 5.4 %collective-permute-start.10 = (f32[1536,128]{1,0:T(8,128)}, f32[1536,128]{1,0:T(8,128)S(1)}, u32[]{:S(2)}, u32[]{:S(2)}) collective-permute-start(f32[1536,128]{1,0:T(8,128)} %get-tuple-element.29), channel_id=1, source_target_pairs={{0,8},{8,0},{32,40},{40,32},{64,72},{72,64},{96,104},{104,96},{16,... | collective-permute-start | bytes 2359304 | tf_op jit(solution)/shard_map/ppermute | solution.py:271
  109.0 21.8 %collective-permute-start.14 = (f32[512,128]{1,0:T(8,128)S(1)}, f32[512,128]{1,0:T(8,128)S(1)}, u32[]{:S(2)}, u32[]{:S(2)}) collective-permute-start(f32[512,128]{1,0:T(8,128)S(1)} %get-tuple-element.36), channel_id=1, source_target_pairs={{0,96},{8,104},{32,0},{40,8},{64,32},{72,40},{96,64},{104,72},{16,... | collective-permute-start | bytes 786440 | tf_op jit(solution)/shard_map/ppermute | solution.py:271
  109.5 21.3 %collective-permute-start.12 = (f32[512,128]{1,0:T(8,128)S(1)}, f32[512,128]{1,0:T(8,128)S(1)}, u32[]{:S(2)}, u32[]{:S(2)}) collective-permute-start(f32[512,128]{1,0:T(8,128)S(1)} %get-tuple-element.37), channel_id=1, source_target_pairs={{0,64},{8,72},{32,96},{40,104},{64,0},{72,8},{96,32},{104,40},{16,... | collective-permute-start | bytes 786440 | tf_op jit(solution)/shard_map/ppermute | solution.py:271
  111.6 19.1 %copy-start.5 = (f32[512]{0:T(512)S(1)}, f32[512]{0:T(512)}, u32[]{:S(2)}) copy-start(f32[512]{0:T(512)} %param.11) | copy-start | bytes 6148
  111.6 20.5 %copy-start.4 = (f32[512,128]{1,0:T(8,128)S(1)}, f32[512,128]{1,0:T(8,128)}, u32[]{:S(2)}) copy-start(f32[512,128]{1,0:T(8,128)} %param.12) | copy-start | bytes 786436
  111.6 19.2 %collective-permute-start.13 = (f32[512,128]{1,0:T(8,128)S(1)}, f32[512,128]{1,0:T(8,128)S(1)}, u32[]{:S(2)}, u32[]{:S(2)}) collective-permute-start(f32[512,128]{1,0:T(8,128)S(1)} %get-tuple-element.35), channel_id=1, source_target_pairs={{0,32},{8,40},{32,64},{40,72},{64,96},{72,104},{96,0},{104,8},{16,... | collective-permute-start | bytes 786440 | tf_op jit(solution)/shard_map/ppermute | solution.py:271
  129.8 2.3 %collective-permute-start.11 = (f32[512,128]{1,0:T(8,128)}, f32[512,128]{1,0:T(8,128)S(1)}, u32[]{:S(2)}, u32[]{:S(2)}) collective-permute-start(f32[512,128]{1,0:T(8,128)} %get-tuple-element.33), channel_id=1, source_target_pairs={{0,8},{8,0},{32,40},{40,32},{64,72},{72,64},{96,104},{104,96},{16,... | collective-permute-start | bytes 786440 | tf_op jit(solution)/shard_map/ppermute | solution.py:271

commit v4 on v3

--- a/solution.py
+++ b/solution.py
@@ -29,7 +29,7 @@
 
 
 def expansions():
-    den, face_row, face_col = (np.zeros((128, SLOTS), np.float32) for _ in range(3))
+    den, face_row, face_col = (np.zeros((PARTS, SLOTS), np.float32) for _ in range(3))
     for i in range(3):
         den[i, i] = -2
         den[ONES, SIZE + i] = 1
@@ -122,7 +122,7 @@
         ),
         scratch_shapes=[
             pltpu.VMEM((8, tiles * TILE), F32),
-            pltpu.VMEM((128, tiles * TILE), F32),
+            pltpu.VMEM((PARTS, tiles * TILE), F32),
             pltpu.VMEM(geom.shape, F32),
         ],
         compiler_params=params(),

time: 134 us -> 134 us (level)
  no operation moved by 1% of the time
where the time goes in v4:
time: 134 us
  Pallas kernels  97.8 us (73%)
  starting transfers between devices  23.8 us (18%)
  local copies, waits for them, and re-layouts  4.86 us (4%)
  other arithmetic  3.75 us (3%)
  waiting for transfers between devices  3.53 us (3%)
    pallas_call x3, Pallas kernels, sweep(): pl.pallas_call(functools.partial(sweep_kernel, first, has_total, split),...  86.2 us
    ppermute x15, starting transfers between devices, shift(): return lax.ppermute(value, AXES, pairs)  23.8 us
    pallas_call x2, Pallas kernels, make_cols(): pl.pallas_call(functools.partial(cols_kernel, dys), out_shape=(jax.ShapeD...  6.09 us
    pallas_call x1, Pallas kernels, make_rows(): pl.pallas_call(rows_kernel, out_shape=(jax.ShapeDtypeStruct((3, tiles * T...  3.69 us
    ppermute x15, waiting for transfers between devices, shift(): return lax.ppermute(value, AXES, pairs)  3.53 us
    unnamed x15, local copies, waits for them, and re-layouts  2.87 us
  transfers between devices with their start and end apart: 15, of which 2 were waited for; matrix products, arithmetic and copies ran while one was open for 2% of the time, Pallas kernels for 35%

profile of v4, /device:TPU:1, one launch (start us, length us, event | category | flops | bytes accessed | tf_op | source)
XLA Modules:
  0.0 133.9 jit_solution(17266567508865560243)
XLA Ops:
  0.0 1.3 broadcast_in_dim.4.area
  1.3 1.8 %shard_map.82 = (bf16[576,128]{1,0:T(8,128)(2,1)}, bf16[64,128]{1,0:T(8,128)(2,1)}) custom-call(bf16[3,512]{1,0:T(4,128)(2,1)} %pos.1, bf16[3,512]{1,0:T(4,128)(2,1)} %nrm.1, bf16[1,512]{1,0:T(2,128)(2,1)} %broadcast_in_dim.4.area, f32[512,128]{1,0:T(8,128)} %rad.1, s32[32,512]{1,0:T(8,128)} %vis.1), custom_call_target="tpu_custom_call" | custom-call | tf_op jit(solution)/shard_map/pallas_call | solution.py:71
  3.0 2.5 %collective-permute-start.2 = (bf16[64,128]{1,0:T(8,128)(2,1)}, bf16[64,128]{1,0:T(8,128)(2,1)S(1)}, u32[]{:S(2)}, u32[]{:S(2)}) collective-permute-start(bf16[64,128]{1,0:T(8,128)(2,1)} %get-tuple-element.20), channel_id=1, source_target_pairs={{0,32},{8,40},{32,64},{40,72},{64,96},{72,104},{96,0},{104,8},{16,... | collective-permute-start | bytes 49160 | tf_op jit(solution)/shard_map/ppermute | solution.py:271
  5.5 3.3 %collective-permute-start.1 = (bf16[64,128]{1,0:T(8,128)(2,1)}, bf16[64,128]{1,0:T(8,128)(2,1)S(1)}, u32[]{:S(2)}, u32[]{:S(2)}) collective-permute-start(bf16[64,128]{1,0:T(8,128)(2,1)} %get-tuple-element.20), channel_id=1, source_target_pairs={{0,64},{8,72},{32,96},{40,104},{64,0},{72,8},{96,32},{104,40},{16,... | collective-permute-start | bytes 49160 | tf_op jit(solution)/shard_map/ppermute | solution.py:271
  8.8 0.7 collective-permute-start
  9.5 2.5 %collective-permute-start.4 = (bf16[576,128]{1,0:T(8,128)(2,1)}, bf16[576,128]{1,0:T(8,128)(2,1)S(1)}, u32[]{:S(2)}, u32[]{:S(2)}) collective-permute-start(bf16[576,128]{1,0:T(8,128)(2,1)} %get-tuple-element.22), channel_id=1, source_target_pairs={{0,3},{8,11},{32,35},{40,43},{64,67},{72,75},{96,99},{104,107},{16... | collective-permute-start | bytes 442376 | tf_op jit(solution)/shard_map/ppermute | solution.py:271
  12.0 0.5 collective-permute-start.5
  12.5 0.0 collective-permute-done.2
  12.5 0.6 collective-permute-start.6
  13.2 0.0 collective-permute-done.1
  13.2 0.0 collective-permute-done
  13.2 0.7 fusion
  13.9 2.4 %collective-permute-start.3 = (bf16[4,64,128]{2,1,0:T(8,128)(2,1)S(1)}, bf16[4,64,128]{2,1,0:T(8,128)(2,1)S(1)}, u32[]{:S(2)}, u32[]{:S(2)}) collective-permute-start(bf16[4,64,128]{2,1,0:T(8,128)(2,1)S(1)} %get-tuple-element.39), channel_id=1, source_target_pairs={{0,8},{8,0},{32,40},{40,32},{64,72},{72,64},{96,104},{104,96},{16,... | collective-permute-start | bytes 196616 | tf_op jit(solution)/shard_map/ppermute | solution.py:271
  16.3 0.9 constant_dynamic-update-slice_fusion.3
  17.3 0.0 collective-permute-done.3
  17.3 0.7 copy.9
  17.9 3.7 %shard_map.83 = (bf16[3,4096,64]{2,1,0:T(8,128)(2,1)}, bf16[4,32,128]{2,1,0:T(8,128)(2,1)}) custom-call(bf16[512,128]{1,0:T(8,128)(2,1)} %bitcast.8, bf16[3,32,64]{2,1,0:T(8,128)(2,1)} %constant.4.clone.expand), custom_call_target="tpu_custom_call" | custom-call | tf_op jit(solution)/shard_map/pallas_call | solution.py:117
  21.6 0.0 collective-permute-done.4
  21.7 0.0 collective-permute-done.5
  21.7 0.0 collective-permute-done.6
  21.8 0.0 copy-start
  21.8 2.8 %collective-permute-start.7 = (bf16[2304,128]{1,0:T(8,128)(2,1)S(1)}, bf16[2304,128]{1,0:T(8,128)(2,1)S(1)}, u32[]{:S(2)}, u32[]{:S(2)}) collective-permute-start(bf16[2304,128]{1,0:T(8,128)(2,1)S(1)} %constant_dynamic-update-slice_fusion.refs_0_), channel_id=1, source_target_pairs={{0,20},{8,28},{32,52},{40,60},{64,84},{72,92},{96,116},{104,124},{... | collective-permute-start | bytes 1769480 | tf_op jit(solution)/shard_map/ppermute | solution.py:271
  24.6 0.0 collective-permute-start.8
  24.6 1.6 %collective-permute-start.9 = (bf16[2304,128]{1,0:T(8,128)(2,1)S(1)}, bf16[2304,128]{1,0:T(8,128)(2,1)S(1)}, u32[]{:S(2)}, u32[]{:S(2)}) collective-permute-start(bf16[2304,128]{1,0:T(8,128)(2,1)S(1)} %constant_dynamic-update-slice_fusion.refs_0_), channel_id=1, source_target_pairs={{0,4},{8,12},{32,36},{40,44},{64,68},{72,76},{96,100},{104,108},{1... | collective-permute-start | bytes 1769480 | tf_op jit(solution)/shard_map/ppermute | solution.py:271
  26.2 0.0 copy-done
  26.2 2.4 %shard_map.85 = (bf16[64,2048]{1,0:T(8,128)(2,1)}, bf16[2048,128]{1,0:T(8,128)(2,1)}) custom-call(bf16[2304,128]{1,0:T(8,128)(2,1)} %copy-done, bf16[4,32,128]{2,1,0:T(8,128)(2,1)} %get-tuple-element.23.refs_3_.refs_1_), custom_call_target="tpu_custom_call" | custom-call | tf_op jit(solution)/shard_map/pallas_call | solution.py:177
  28.6 22.1 %shard_map.86.refs_3_ = f32[4096,128]{1,0:T(8,128)} custom-call(bf16[3,4096,64]{2,1,0:T(8,128)(2,1)} %get-tuple-element.21.refs_0_, bf16[64,2048]{1,0:T(8,128)(2,1)} %get-tuple-element.26.refs_1_, bf16[2048,128]{1,0:T(8,128)(2,1)} %get-tuple-element.27.refs_2_), custom_call_target="tpu_custom_call" | custom-call | flops 25769803776 | bytes 1048576 | tf_op jit(solution)/shard_map/pallas_call | solution.py:247
  50.7 0.0 collective-permute-done.7.refs_0_
  50.7 0.0 copy-start.1
  50.7 0.0 collective-permute-done.8.refs_1_
  50.7 0.0 copy-start.2
  50.7 0.0 collective-permute-done.9.refs_2_
  50.7 0.9 copy-done.1
  51.6 0.2 copy-done.2
  51.8 0.0 copy-start.3
  51.8 0.8 copy-done.3
  52.6 3.7 %shard_map.84 = (bf16[64,6144]{1,0:T(8,128)(2,1)}, bf16[6144,128]{1,0:T(8,128)(2,1)}) custom-call(bf16[2304,128]{1,0:T(8,128)(2,1)} %copy-done.1, bf16[2304,128]{1,0:T(8,128)(2,1)} %copy-done.2, bf16[2304,128]{1,0:T(8,128)(2,1)} %copy-done.3, bf16[4,32,128]{2,1,0:T(8,128)(2,1)} %get-tuple-element.23.refs_3_.refs_1_), custom_call_target="tpu_custom_call" | custom-call | tf_op jit(solution)/shard_map/pallas_call | solution.py:177
  56.3 45.9 %shard_map.87 = (f32[1536,128]{1,0:T(8,128)}, f32[1536,128]{1,0:T(8,128)}) custom-call(bf16[3,4096,64]{2,1,0:T(8,128)(2,1)} %get-tuple-element.21.refs_0_, bf16[64,6144]{1,0:T(8,128)(2,1)} %get-tuple-element.30.refs_1_, bf16[6144,128]{1,0:T(8,128)(2,1)} %get-tuple-element.31.refs_2_, f32[4096,128]{1,0:T(8,128)} %shard_map.86.refs_3_), custom_call_target="tpu_custom_call" | custom-call | flops 57982058496 | bytes 1048576 | tf_op jit(solution)/shard_map/pallas_call | solution.py:247
  102.3 3.3 %collective-permute-start.10 = (f32[1536,128]{1,0:T(8,128)}, f32[1536,128]{1,0:T(8,128)S(1)}, u32[]{:S(2)}, u32[]{:S(2)}) collective-permute-start(f32[1536,128]{1,0:T(8,128)} %get-tuple-element.29), channel_id=1, source_target_pairs={{0,8},{8,0},{32,40},{40,32},{64,72},{72,64},{96,104},{104,96},{16,... | collective-permute-start | bytes 2359304 | tf_op jit(solution)/shard_map/ppermute | solution.py:271
  105.5 2.1 %collective-permute-done.10 = f32[1536,128]{1,0:T(8,128)S(1)} collective-permute-done((f32[1536,128]{1,0:T(8,128)}, f32[1536,128]{1,0:T(8,128)S(1)}, u32[]{:S(2)}, u32[]{:S(2)}) %collective-permute-start.10) | collective-permute-done | bytes 786464 | tf_op jit(solution)/shard_map/ppermute | solution.py:271
  107.7 1.2 add.18
  108.9 0.1 fusion.1
  108.9 0.5 collective-permute-start.14
  109.4 2.1 %collective-permute-start.12 = (f32[512,128]{1,0:T(8,128)S(1)}, f32[512,128]{1,0:T(8,128)S(1)}, u32[]{:S(2)}, u32[]{:S(2)}) collective-permute-start(f32[512,128]{1,0:T(8,128)S(1)} %get-tuple-element.37), channel_id=1, source_target_pairs={{0,64},{8,72},{32,96},{40,104},{64,0},{72,8},{96,32},{104,40},{16,... | collective-permute-start | bytes 786440 | tf_op jit(solution)/shard_map/ppermute | solution.py:271
  111.5 0.0 copy-start.5
  111.6 0.0 copy-start.4
  111.6 0.0 collective-permute-start.13
  111.6 18.2 %shard_map.88 = (f32[512,128]{1,0:T(8,128)}, f32[512,128]{1,0:T(8,128)}) custom-call(bf16[3,4096,64]{2,1,0:T(8,128)(2,1)} %get-tuple-element.21.refs_0_, bf16[64,6144]{1,0:T(8,128)(2,1)} %get-tuple-element.30.refs_1_, bf16[6144,128]{1,0:T(8,128)(2,1)} %get-tuple-element.31.refs_2_, f32[4096,128]{1,0:T(8,128)} %shard_map.86.refs_3_), custom_call_target="tpu_custom_call" | custom-call | flops 19327352832 | bytes 1048576 | tf_op jit(solution)/shard_map/pallas_call | solution.py:247
  129.8 0.9 collective-permute-start.11
  130.7 0.0 copy-done.5
  130.7 0.0 collective-permute-done.14
  130.7 0.0 collective-permute-done.12
  130.7 0.0 collective-permute-done.13
  130.7 1.3 %collective-permute-done.11 = f32[512,128]{1,0:T(8,128)S(1)} collective-permute-done((f32[512,128]{1,0:T(8,128)}, f32[512,128]{1,0:T(8,128)S(1)}, u32[]{:S(2)}, u32[]{:S(2)}) %collective-permute-start.11) | collective-permute-done | bytes 262176 | tf_op jit(solution)/shard_map/ppermute | solution.py:271
  132.1 0.0 copy-done.4
  132.1 1.8 %multiply_add_fusion = f32[512,128]{1,0:T(8,128)} fusion(f32[512,128]{1,0:T(8,128)S(1)} %copy-done.4, f32[512,128]{1,0:T(8,128)S(1)} %collective-permute-done.14, f32[512,128]{1,0:T(8,128)S(1)} %collective-permute-done.12, f32[512,128]{1,0:T(8,128)S(1)} %collective-permute-done.13, f32[512,128]{1,0:T(8,128)} %get-tuple-element.32, ...), kind=kLoop, calls=%fused_computation | loop fusion | flops 393216 | bytes 1837056 | tf_op jit(solution)/shard_map/add | solution.py:292
  (5 shorter events, 0.1 us)
Async XLA Ops:
  3.0 9.5 %collective-permute-start.2 = (bf16[64,128]{1,0:T(8,128)(2,1)}, bf16[64,128]{1,0:T(8,128)(2,1)S(1)}, u32[]{:S(2)}, u32[]{:S(2)}) collective-permute-start(bf16[64,128]{1,0:T(8,128)(2,1)} %get-tuple-element.20), channel_id=1, source_target_pairs={{0,32},{8,40},{32,64},{40,72},{64,96},{72,104},{96,0},{104,8},{16,... | collective-permute-start | bytes 49160 | tf_op jit(solution)/shard_map/ppermute | solution.py:271
  5.5 7.6 %collective-permute-start.1 = (bf16[64,128]{1,0:T(8,128)(2,1)}, bf16[64,128]{1,0:T(8,128)(2,1)S(1)}, u32[]{:S(2)}, u32[]{:S(2)}) collective-permute-start(bf16[64,128]{1,0:T(8,128)(2,1)} %get-tuple-element.20), channel_id=1, source_target_pairs={{0,64},{8,72},{32,96},{40,104},{64,0},{72,8},{96,32},{104,40},{16,... | collective-permute-start | bytes 49160 | tf_op jit(solution)/shard_map/ppermute | solution.py:271
  8.8 4.3 %collective-permute-start = (bf16[64,128]{1,0:T(8,128)(2,1)}, bf16[64,128]{1,0:T(8,128)(2,1)S(1)}, u32[]{:S(2)}, u32[]{:S(2)}) collective-permute-start(bf16[64,128]{1,0:T(8,128)(2,1)} %get-tuple-element.20), channel_id=1, source_target_pairs={{0,96},{8,104},{32,0},{40,8},{64,32},{72,40},{96,64},{104,72},{16,... | collective-permute-start | bytes 49160 | tf_op jit(solution)/shard_map/ppermute | solution.py:271
  9.5 12.1 %collective-permute-start.4 = (bf16[576,128]{1,0:T(8,128)(2,1)}, bf16[576,128]{1,0:T(8,128)(2,1)S(1)}, u32[]{:S(2)}, u32[]{:S(2)}) collective-permute-start(bf16[576,128]{1,0:T(8,128)(2,1)} %get-tuple-element.22), channel_id=1, source_target_pairs={{0,3},{8,11},{32,35},{40,43},{64,67},{72,75},{96,99},{104,107},{16... | collective-permute-start | bytes 442376 | tf_op jit(solution)/shard_map/ppermute | solution.py:271
  12.0 9.6 %collective-permute-start.5 = (bf16[576,128]{1,0:T(8,128)(2,1)}, bf16[576,128]{1,0:T(8,128)(2,1)S(1)}, u32[]{:S(2)}, u32[]{:S(2)}) collective-permute-start(bf16[576,128]{1,0:T(8,128)(2,1)} %get-tuple-element.22), channel_id=1, source_target_pairs={{0,2},{8,10},{32,34},{40,42},{64,66},{72,74},{96,98},{104,106},{16... | collective-permute-start | bytes 442376 | tf_op jit(solution)/shard_map/ppermute | solution.py:271
  12.5 9.2 %collective-permute-start.6 = (bf16[576,128]{1,0:T(8,128)(2,1)}, bf16[576,128]{1,0:T(8,128)(2,1)S(1)}, u32[]{:S(2)}, u32[]{:S(2)}) collective-permute-start(bf16[576,128]{1,0:T(8,128)(2,1)} %get-tuple-element.22), channel_id=1, source_target_pairs={{0,1},{8,9},{32,33},{40,41},{64,65},{72,73},{96,97},{104,105},{16,... | collective-permute-start | bytes 442376 | tf_op jit(solution)/shard_map/ppermute | solution.py:271
  13.9 3.4 %collective-permute-start.3 = (bf16[4,64,128]{2,1,0:T(8,128)(2,1)S(1)}, bf16[4,64,128]{2,1,0:T(8,128)(2,1)S(1)}, u32[]{:S(2)}, u32[]{:S(2)}) collective-permute-start(bf16[4,64,128]{2,1,0:T(8,128)(2,1)S(1)} %get-tuple-element.39), channel_id=1, source_target_pairs={{0,8},{8,0},{32,40},{40,32},{64,72},{72,64},{96,104},{104,96},{16,... | collective-permute-start | bytes 196616 | tf_op jit(solution)/shard_map/ppermute | solution.py:271
  21.8 4.5 %copy-start = (bf16[2304,128]{1,0:T(8,128)(2,1)}, bf16[2304,128]{1,0:T(8,128)(2,1)S(1)}, u32[]{:S(2)}) copy-start(bf16[2304,128]{1,0:T(8,128)(2,1)S(1)} %constant_dynamic-update-slice_fusion.refs_0_) | copy-start | bytes 1769476
  21.8 28.9 %collective-permute-start.7 = (bf16[2304,128]{1,0:T(8,128)(2,1)S(1)}, bf16[2304,128]{1,0:T(8,128)(2,1)S(1)}, u32[]{:S(2)}, u32[]{:S(2)}) collective-permute-start(bf16[2304,128]{1,0:T(8,128)(2,1)S(1)} %constant_dynamic-update-slice_fusion.refs_0_), channel_id=1, source_target_pairs={{0,20},{8,28},{32,52},{40,60},{64,84},{72,92},{96,116},{104,124},{... | collective-permute-start | bytes 1769480 | tf_op jit(solution)/shard_map/ppermute | solution.py:271
  24.6 26.1 %collective-permute-start.8 = (bf16[2304,128]{1,0:T(8,128)(2,1)S(1)}, bf16[2304,128]{1,0:T(8,128)(2,1)S(1)}, u32[]{:S(2)}, u32[]{:S(2)}) collective-permute-start(bf16[2304,128]{1,0:T(8,128)(2,1)S(1)} %constant_dynamic-update-slice_fusion.refs_0_), channel_id=1, source_target_pairs={{0,16},{8,24},{32,48},{40,56},{64,80},{72,88},{96,112},{104,120},{... | collective-permute-start | bytes 1769480 | tf_op jit(solution)/shard_map/ppermute | solution.py:271
  24.6 26.1 %collective-permute-start.9 = (bf16[2304,128]{1,0:T(8,128)(2,1)S(1)}, bf16[2304,128]{1,0:T(8,128)(2,1)S(1)}, u32[]{:S(2)}, u32[]{:S(2)}) collective-permute-start(bf16[2304,128]{1,0:T(8,128)(2,1)S(1)} %constant_dynamic-update-slice_fusion.refs_0_), channel_id=1, source_target_pairs={{0,4},{8,12},{32,36},{40,44},{64,68},{72,76},{96,100},{104,108},{1... | collective-permute-start | bytes 1769480 | tf_op jit(solution)/shard_map/ppermute | solution.py:271
  50.7 0.9 copy-start.1
  50.7 1.1 copy-start.2
  51.8 0.8 copy-start.3
  102.3 5.4 %collective-permute-start.10 = (f32[1536,128]{1,0:T(8,128)}, f32[1536,128]{1,0:T(8,128)S(1)}, u32[]{:S(2)}, u32[]{:S(2)}) collective-permute-start(f32[1536,128]{1,0:T(8,128)} %get-tuple-element.29), channel_id=1, source_target_pairs={{0,8},{8,0},{32,40},{40,32},{64,72},{72,64},{96,104},{104,96},{16,... | collective-permute-start | bytes 2359304 | tf_op jit(solution)/shard_map/ppermute | solution.py:271
  108.9 21.8 %collective-permute-start.14 = (f32[512,128]{1,0:T(8,128)S(1)}, f32[512,128]{1,0:T(8,128)S(1)}, u32[]{:S(2)}, u32[]{:S(2)}) collective-permute-start(f32[512,128]{1,0:T(8,128)S(1)} %get-tuple-element.36), channel_id=1, source_target_pairs={{0,96},{8,104},{32,0},{40,8},{64,32},{72,40},{96,64},{104,72},{16,... | collective-permute-start | bytes 786440 | tf_op jit(solution)/shard_map/ppermute | solution.py:271
  109.4 21.3 %collective-permute-start.12 = (f32[512,128]{1,0:T(8,128)S(1)}, f32[512,128]{1,0:T(8,128)S(1)}, u32[]{:S(2)}, u32[]{:S(2)}) collective-permute-start(f32[512,128]{1,0:T(8,128)S(1)} %get-tuple-element.37), channel_id=1, source_target_pairs={{0,64},{8,72},{32,96},{40,104},{64,0},{72,8},{96,32},{104,40},{16,... | collective-permute-start | bytes 786440 | tf_op jit(solution)/shard_map/ppermute | solution.py:271
  111.5 19.1 %copy-start.5 = (f32[512]{0:T(512)S(1)}, f32[512]{0:T(512)}, u32[]{:S(2)}) copy-start(f32[512]{0:T(512)} %param.11) | copy-start | bytes 6148
  111.6 20.5 %copy-start.4 = (f32[512,128]{1,0:T(8,128)S(1)}, f32[512,128]{1,0:T(8,128)}, u32[]{:S(2)}) copy-start(f32[512,128]{1,0:T(8,128)} %param.12) | copy-start | bytes 786436
  111.6 19.2 %collective-permute-start.13 = (f32[512,128]{1,0:T(8,128)S(1)}, f32[512,128]{1,0:T(8,128)S(1)}, u32[]{:S(2)}, u32[]{:S(2)}) collective-permute-start(f32[512,128]{1,0:T(8,128)S(1)} %get-tuple-element.35), channel_id=1, source_target_pairs={{0,32},{8,40},{32,64},{40,72},{64,96},{72,104},{96,0},{104,8},{16,... | collective-permute-start | bytes 786440 | tf_op jit(solution)/shard_map/ppermute | solution.py:271
  129.8 2.3 %collective-permute-start.11 = (f32[512,128]{1,0:T(8,128)}, f32[512,128]{1,0:T(8,128)S(1)}, u32[]{:S(2)}, u32[]{:S(2)}) collective-permute-start(f32[512,128]{1,0:T(8,128)} %get-tuple-element.33), channel_id=1, source_target_pairs={{0,8},{8,0},{32,40},{40,32},{64,72},{72,64},{96,104},{104,96},{16,... | collective-permute-start | bytes 786440 | tf_op jit(solution)/shard_map/ppermute | solution.py:271
